TPU v7x, 256 devices: a whole 4x4x8 slice. The times are simulated.
256 devices in a mesh: ep: 32 (over x_lo, z, core), tp: 8 (over x_hi, y).
Axes of the slice: x: 4 (x_hi: 2, x_lo: 2; x = x_hi * 2 + x_lo), y: 4, z: 8, core: 2. Of those that a mesh axis runs over, the one named last changes fastest.
Arguments:
- residual_in: bfloat16 [6144, 2048], P('ep'), may hold values from -6 to 6
- shortcut: bfloat16 [6144, 2048], P('ep'), may hold values from -6 to 6
- attn_gain: float32 [2048], replicated, may hold values from 0.25 to 1.75
- moe_gain: float32 [2048], replicated, may hold values from 0.25 to 1.75
- query_weight: bfloat16 [2048, 4096], P('ep', 'tp')
- key_value: bfloat16 [2048, 1024], P('ep')
- output_weight: bfloat16 [2048, 4096], P('ep', 'tp'), may hold values from -0.09375 to 0.09375
- query_gain: float32 [128], replicated, may hold values from 0.5 to 5
- key_gain: float32 [128], replicated, may hold values from 0.5 to 5
- router_weight: bfloat16 [128, 2048], replicated, may hold values from -0.125 to 0.125
- expert_ids: int32 [6144, 8], P('ep'), may hold values from 0 to 127, all different within a row; in each aligned block of 192 rows (0 to 191, 192 to 383, ...) at most 15 rows name the same one
- gate_up_weight: bfloat16 [256, 2048, 1536], P(('ep', 'tp')), may hold values from -0.125 to 0.125
- down_weight: bfloat16 [256, 768, 2048], P(('ep', 'tp')), may hold values from -0.15625 to 0.15625
Outputs:
- layer_out: bfloat16 [6144, 2048], P('ep')
Inputs may be any that keep to these rules, and one draw needn't show every extreme that they name: `expert_ids`: each row names 8 different experts. Among the 192 rows of one sequence no expert is named by more than 15 rows, a bound that some block reaches.
All inputs are finite; a program needn't handle non-finite values.
Results may differ from a plain program's by a relative error of at most 0.009.
Values may be sent and summed in bfloat16 or wider, within the bound.
No kernel may reach another device: no remote copies, remote signals or barrier semaphores. Data moves between devices by JAX's collectives and lax.ppermute only.
A program may use at most 128 MiB of HBM per device.

v0:
```python
import jax
import jax.numpy as jnp
from jax import lax
from jax.sharding import PartitionSpec as P

HD = 128
QH = 32
KVH = 4
TOPK = 8


EPS = 1e-06
ROPE_BASE = 1000000.0


def from_partner(value, axis, apart):
    mask = 2**apart
    pairs = [(source, source ^ mask) for source in range(lax.axis_size(axis))]
    return lax.ppermute(value, axis, pairs)


def norm_rows(values, gain):
    wide = values.astype(jnp.float32)
    return wide * lax.rsqrt(jnp.mean(wide * wide, -1, keepdims=True) + EPS) * gain


def rotary(values):
    length = values.shape[0]
    half = values.shape[-1] // 2
    position = jnp.arange(length, dtype=jnp.float32)
    freq = ROPE_BASE ** (-jnp.arange(half, dtype=jnp.float32) * 2.0 / values.shape[-1])
    angle = position[:, None] * freq[None, :]
    cosine = jnp.cos(angle)[:, None, :]
    sine = jnp.sin(angle)[:, None, :]
    first = values[..., :half]
    second = values[..., half:]
    return jnp.concatenate([first * cosine - second * sine, second * cosine + first * sine], -1)


def capacity_of(rows, experts):
    return max(2, 5 * rows * TOPK // (4 * experts))


def attend(query, keyval, query_gain, key_gain, kv_count):
    seq = query.shape[0]
    query = rotary(norm_rows(query.reshape(seq, -1, HD), query_gain)).astype(jnp.bfloat16)
    heads = query.shape[1]
    query = query.reshape(seq, kv_count, heads // kv_count, HD)
    keyval = keyval.reshape(seq, 2, kv_count, HD)
    keys = rotary(norm_rows(keyval[:, 0], key_gain)).astype(jnp.bfloat16)
    values = keyval[:, 1].astype(jnp.bfloat16)
    logits = jnp.einsum("sgjd,tgd->gjst", query, keys, preferred_element_type=jnp.float32) * HD ** (
        -0.5
    )
    causal = jnp.arange(seq)[:, None] >= jnp.arange(seq)[None, :]
    logits = jnp.where(causal, logits, -1e30)
    peak = jnp.max(logits, -1, keepdims=True)
    expo = jnp.exp(logits - peak)
    probs = (expo / jnp.sum(expo, -1, keepdims=True)).astype(jnp.bfloat16)
    attended = jnp.einsum("gjst,tgd->sgjd", probs, values, preferred_element_type=jnp.float32)
    return attended.astype(jnp.bfloat16).reshape(seq, heads * HD)


def project_out(attended, weight):
    return lax.dot_general(
        attended, weight, (((1,), (1,)), ((), ())), preferred_element_type=jnp.float32
    )


def local(
    residual_in,
    shortcut,
    attn_gain,
    moe_gain,
    query_weight,
    key_value,
    output_weight,
    query_gain,
    key_gain,
    router_weight,
    expert_ids,
    gate_up_weight,
    down_weight,
):
    n_ep = lax.axis_size("ep")
    n_tp = lax.axis_size("tp")
    rank = lax.axis_index("tp")
    pairs = n_tp // 2
    group_id = rank // 2
    side = rank % 2
    rows, d_model = residual_in.shape
    half_width = d_model // 2
    experts = router_weight.shape[0]
    capacity = capacity_of(rows, experts)
    ff_dev = down_weight.shape[1]
    qh_dev = query_weight.shape[1] // HD
    group = QH // KVH
    kv_count = max(1, qh_dev // group)
    kv_start = rank * qh_dev // group
    attn_rows = norm_rows(residual_in, attn_gain).astype(jnp.bfloat16)
    moe_rows = norm_rows(shortcut, moe_gain).astype(jnp.bfloat16)
    logits_router = lax.dot_general(
        moe_rows, router_weight, (((1,), (1,)), ((), ())), preferred_element_type=jnp.float32
    )
    hits = (expert_ids[:, :, None] == jnp.arange(experts, dtype=jnp.int32)[None, None, :]).astype(
        jnp.float32
    )
    chosen = jnp.sum(hits * logits_router[:, None, :], -1)
    scores = jax.nn.sigmoid(chosen)
    gates = (scores / jnp.sum(scores, 1, keepdims=True)).astype(jnp.bfloat16)
    per_row = jnp.sum(hits, 1).astype(jnp.bfloat16)
    lower = (jnp.arange(rows)[:, None] > jnp.arange(rows)[None, :]).astype(jnp.bfloat16)
    earlier = jnp.dot(lower, per_row, preferred_element_type=jnp.float32)
    slot = jnp.sum(hits * earlier[:, None, :], -1)
    mine = expert_ids % pairs == group_id
    target = (expert_ids // pairs).astype(jnp.float32) * capacity + slot
    target = jnp.where(mine, target, -1.0)
    places = jnp.arange(n_ep * capacity, dtype=jnp.float32)
    match = (target[:, :, None] == places[None, None, :]).astype(jnp.float32)
    dispatch_map = jnp.sum(match, 1).astype(jnp.bfloat16)
    combine = jnp.sum(match * gates.astype(jnp.float32)[:, :, None], 1).astype(jnp.bfloat16)
    outgoing = lax.dot_general(
        dispatch_map, moe_rows, (((0,), (0,)), ((), ())), preferred_element_type=jnp.float32
    ).astype(jnp.bfloat16)
    outgoing = outgoing.reshape(n_ep, capacity, d_model)
    arrived = lax.all_to_all(outgoing, "ep", split_axis=0, concat_axis=0, tiled=True)
    paired = jnp.einsum(
        "ack,kf->acf", arrived, gate_up_weight[0], preferred_element_type=jnp.float32
    )
    hidden = (jax.nn.silu(paired[..., :ff_dev]) * paired[..., ff_dev:]).astype(jnp.bfloat16)
    partial_sum = jnp.einsum(
        "acf,fk->ack", hidden, down_weight[0], preferred_element_type=jnp.float32
    )
    kept = lax.dynamic_slice_in_dim(partial_sum, side * half_width, half_width, 2)
    handed = lax.dynamic_slice_in_dim(partial_sum, (1 - side) * half_width, half_width, 2)
    received = from_partner(handed.astype(jnp.bfloat16), "tp", 0).astype(handed.dtype)
    expert_out = (kept + received).astype(jnp.bfloat16)
    returned = lax.all_to_all(expert_out, "ep", split_axis=0, concat_axis=0, tiled=True).reshape(
        -1, half_width
    )
    moe_cols = jnp.dot(combine, returned, preferred_element_type=jnp.float32)
    blank = jnp.zeros_like(moe_cols)
    moe_full = jnp.where(
        side == 0, jnp.concatenate([moe_cols, blank], 1), jnp.concatenate([blank, moe_cols], 1)
    )
    local_rows = key_value.shape[0]
    local_kv = lax.dynamic_slice_in_dim(
        key_value.reshape(local_rows, 2, KVH, HD), kv_start, kv_count, 2
    )
    local_kv = local_kv.reshape(local_rows, 2 * kv_count * HD)
    full_query, full_kv, full_out = (
        lax.all_gather(query_weight, "ep", axis=0, tiled=True),
        lax.all_gather(local_kv, "ep", axis=0, tiled=True),
        lax.all_gather(output_weight, "ep", axis=0, tiled=True),
    )
    query = jnp.dot(attn_rows, full_query, preferred_element_type=jnp.float32)
    keyval = jnp.dot(attn_rows, full_kv, preferred_element_type=jnp.float32)
    attended = attend(query, keyval, query_gain, key_gain, kv_count)
    attn_terms = project_out(attended, full_out)
    attn_part = attn_terms.astype(jnp.bfloat16).astype(jnp.float32)
    total = attn_part + moe_full
    summed = lax.psum(total, "tp")
    return (residual_in.astype(jnp.float32) + summed).astype(jnp.bfloat16)


def solution(mesh):
    return jax.shard_map(
        local,
        mesh=mesh,
        in_specs=(
            P("ep", None),
            P("ep", None),
            P(),
            P(),
            P("ep", "tp"),
            P("ep", None),
            P("ep", "tp"),
            P(),
            P(),
            P(),
            P("ep", None),
            P(("ep", "tp"), None, None),
            P(("ep", "tp"), None, None),
        ),
        out_specs=P("ep", None),
        check_vma=False,
    )
```

profile of v0, /device:TPU:32, one launch (start us, length us, event | category | flops | bytes accessed | tf_op | source)
XLA Modules:
  0.0 331.5 jit_solution(15880107389892363726)
XLA Ops:
  6.5 1.1 reshape.270
  7.7 0.2 dynamic-slice_reduce_fusion
  7.9 0.6 copy.97
  8.6 0.7 all-gather.6.cloned.1.call-update
  9.3 0.8 copy.64
  10.1 1.4 fusion.7
  11.5 1.7 fusion.28
  13.2 0.6 select_reduce_fusion.1
  13.8 0.1 fusion.38
  14.0 0.5 select_reduce_fusion.2
  14.8 2.5 select_reduce_fusion
  17.4 3.2 convolution_convert_fusion
  20.6 2.8 reshape.276
  23.4 9.7 %all-to-all-start = ((bf16[32,15,2048]{2,1,0:T(8,128)(2,1)}), bf16[32,15,2048]{2,1,0:T(8,128)(2,1)}, u32[]{:S(2)}, u32[]{:S(2)}) async-start(bf16[32,15,2048]{2,1,0:T(8,128)(2,1)} %reshape.276), calls=%async_computation | async-start | bytes 4194304 | tf_op jit(solution)/shard_map/all_to_all | solution.py:126
  33.2 0.7 all-gather.8.cloned.1.call-update
  33.9 1.4 fusion.10
  35.3 1.1 fusion.45
  36.3 52.2 %all-to-all-done = bf16[32,15,2048]{2,1,0:T(8,128)(2,1)} async-done(((bf16[32,15,2048]{2,1,0:T(8,128)(2,1)}), bf16[32,15,2048]{2,1,0:T(8,128)(2,1)}, u32[]{:S(2)}, u32[]{:S(2)}) %all-to-all-start) | async-done | bytes 1966112 | tf_op jit(solution)/shard_map/all_to_all | solution.py:126
  88.6 7.9 %fusion = f32[32,15,1536]{2,0,1:T(8,128)S(1)} fusion(bf16[1,2048,1536]{2,1,0:T(8,128)(2,1)} %param.24, bf16[32,15,2048]{2,1,0:T(8,128)(2,1)} %all-to-all-done), kind=kOutput, calls=%fused_computation | convolution fusion | flops 3019898880 | bytes 11206656 | tf_op jit(solution)/shard_map/ack,kf->acf/dot_general | solution.py:127
  96.5 1.7 fusion.2
  98.2 1.9 copy-done.1
  100.2 1.1 dynamic-slice_convert_fusion
  101.3 1.6 collective-permute-start
  102.9 0.6 iota_compare_fusion.3
  103.5 1.9 fusion.25
  105.6 0.7 slice.33
  106.6 18.4 %collective-permute-done = bf16[32,15,1024]{2,0,1:T(8,128)(2,1)} collective-permute-done((bf16[32,15,1024]{2,0,1:T(8,128)(2,1)}, bf16[32,15,1024]{2,0,1:T(8,128)(2,1)}, u32[]{:S(2)}, u32[]{:S(2)}) %collective-permute-start) | collective-permute-done | bytes 983072 | tf_op jit(solution)/shard_map/ppermute | solution.py:19
  125.0 2.2 add_convert_fusion
  127.2 1.5 copy.72
  128.7 4.5 %all-to-all-start.1 = ((bf16[32,15,1024]{2,1,0:T(8,128)(2,1)}), bf16[32,15,1024]{2,1,0:T(8,128)(2,1)}, u32[]{:S(2)}, u32[]{:S(2)}) async-start(bf16[32,15,1024]{2,1,0:T(8,128)(2,1)} %copy.72), calls=%async_computation.1 | async-start | bytes 2097152 | tf_op jit(solution)/shard_map/all_to_all | solution.py:138
  133.2 1.1 fusion.55
  134.3 21.8 %all-gather.6.cloned.1.call-done = bf16[2048,512]{1,0:T(8,128)(2,1)} async-done(((bf16[64,512]{1,0:T(8,128)(2,1)}), bf16[2048,512]{1,0:T(8,128)(2,1)}) %all-gather.6.cloned.1.call-update) | async-done | bytes 2097168 | tf_op jit(solution)/shard_map/all_gather | solution.py:152
  156.1 2.5 fusion.23
  158.5 0.9 reshape.273
  159.4 1.9 multiply_reduce_fusion
  161.3 1.0 copy.60
  162.3 0.2 fusion.21
  162.5 1.2 subtract_convert_fusion
  163.7 0.4 fusion.60
  164.1 0.1 fusion.20
  164.2 0.4 fusion.17
  164.6 0.2 copy.63
  164.8 2.4 reshape.277
  167.1 2.5 fusion.61
  169.6 52.5 %all-gather.8.cloned.1.call-done = bf16[2048,512]{1,0:T(8,128)(2,1)} async-done(((bf16[64,512]{1,0:T(8,128)(2,1)}), bf16[2048,512]{1,0:T(8,128)(2,1)}) %all-gather.8.cloned.1.call-update) | async-done | bytes 2097168 | tf_op jit(solution)/shard_map/all_gather | solution.py:154
  222.1 4.1 %fusion.5 = f32[192,2048]{1,0:T(8,128)} fusion(bf16[2048,512]{1,0:T(8,128)(2,1)} %all-gather.8.cloned.1.call-done, f32[192,1024]{1,0:T(8,128)} %fusion.61, pred[]{:T(512)S(6)} %eq.39, bf16[24,8,4,128]{3,2,1,0:T(4,128)(2,1)S(1)} %bitcast.66), kind=kOutput, calls=%fused_computation.10 | convolution fusion | flops 404226048 | bytes 4653057 | tf_op jit(solution)/shard_map/dot_general | solution.py:65
  226.2 96.1 %all-reduce.4.cloned.1.call-done = f32[192,2048]{1,0:T(8,128)} async-done(((f32[192,2048]{1,0:T(8,128)}), f32[192,2048]{1,0:T(8,128)}) %all-reduce.4.cloned.1.call-update) | async-done | bytes 1572880 | tf_op jit(solution)/shard_map/psum | solution.py:162
  322.3 2.7 fusion.13
  (43 shorter events, 0.9 us)
Async XLA Ops:
  6.5 89.9 %copy-start = (bf16[1,768,2048]{2,1,0:T(8,128)(2,1)S(1)}, bf16[1,768,2048]{2,1,0:T(8,128)(2,1)}, u32[]{:S(2)}) copy-start(bf16[1,768,2048]{2,1,0:T(8,128)(2,1)} %param.25) | copy-start | bytes 9437188
  6.5 97.0 %all-gather.4.cloned.1.call-start = ((), (), s32[]{:S(2)}) async-start(), calls=%async_computation.2 | async-start | bytes 1081344 | tf_op jit(solution)/shard_map/all_gather | solution.py:153
  8.5 147.5 %all-gather.6.cloned.1.call-start = ((), (), s32[]{:S(2)}) async-start(), calls=%async_computation.3 | async-start | bytes 2162688 | tf_op jit(solution)/shard_map/all_gather | solution.py:152
  11.5 5.9 %copy-start.7 = (f32[2048]{0:T(1024)S(1)}, f32[2048]{0:T(1024)}, u32[]{:S(2)}) copy-start(f32[2048]{0:T(1024)} %param.16) | copy-start | bytes 24580
  23.4 65.1 %all-to-all-start = ((bf16[32,15,2048]{2,1,0:T(8,128)(2,1)}), bf16[32,15,2048]{2,1,0:T(8,128)(2,1)}, u32[]{:S(2)}, u32[]{:S(2)}) async-start(bf16[32,15,2048]{2,1,0:T(8,128)(2,1)} %reshape.276), calls=%async_computation | async-start | bytes 4194304 | tf_op jit(solution)/shard_map/all_to_all | solution.py:126
  33.1 188.9 %all-gather.8.cloned.1.call-start = ((), (), s32[]{:S(2)}) async-start(), calls=%async_computation.4 | async-start | bytes 2162688 | tf_op jit(solution)/shard_map/all_gather | solution.py:154
  98.2 2.0 copy-start.1
  100.2 3.3 %copy-start.10 = (f32[2048]{0:T(1024)S(1)}, f32[2048]{0:T(1024)}, u32[]{:S(2)}) copy-start(f32[2048]{0:T(1024)} %param.15) | copy-start | bytes 24580
  101.3 23.7 %collective-permute-start = (bf16[32,15,1024]{2,0,1:T(8,128)(2,1)}, bf16[32,15,1024]{2,0,1:T(8,128)(2,1)}, u32[]{:S(2)}, u32[]{:S(2)}) collective-permute-start(bf16[32,15,1024]{2,0,1:T(8,128)(2,1)} %dynamic-slice_convert_fusion), channel_id=1, source_target_pairs={{0,1},{1,0},{2,3},{3,2},{4,5},{5,4},{6,7},{7,6},{8,9},{9,8},{10,11... | collective-permute-start | bytes 2949128 | tf_op jit(solution)/shard_map/ppermute | solution.py:19
  103.5 3.0 copy-start.8
  128.7 36.1 %all-to-all-start.1 = ((bf16[32,15,1024]{2,1,0:T(8,128)(2,1)}), bf16[32,15,1024]{2,1,0:T(8,128)(2,1)}, u32[]{:S(2)}, u32[]{:S(2)}) async-start(bf16[32,15,1024]{2,1,0:T(8,128)(2,1)} %copy.72), calls=%async_computation.1 | async-start | bytes 2097152 | tf_op jit(solution)/shard_map/all_to_all | solution.py:138
  133.2 189.1 %all-reduce.4.cloned.1.call-start = ((), (), s32[]{:S(2)}) async-start(), calls=%async_computation.5 | async-start | bytes 3145728 | tf_op jit(solution)/shard_map/psum | solution.py:162
  134.3 28.1 %copy-start.9 = (f32[128]{0:T(128)S(1)}, f32[128]{0:T(128)}, u32[]{:S(2)}) copy-start(f32[128]{0:T(128)} %param.20) | copy-start | bytes 1540
  162.3 1.4 copy-start.3
  162.3 1.4 copy-start.4
  162.3 1.4 copy-start.5
  162.5 1.7 copy-start.6
  164.6 2.5 copy-start.2
Sparse Core Ops, SparseCore 0:
  9.2 73.8 all-gather.3
  85.0 70.9 all-gather.5
  157.9 64.1 all-gather.7
  226.3 95.9 all-reduce.3
where the time goes:
time: 332 us; the launch traced here: 331 us
  waiting for transfers between devices  242 us (73%)
  matrix products  26.4 us (8%)
  other arithmetic  17.7 us (5%)
  starting transfers between devices  15.9 us (5%)
  local copies, waits for them, and re-layouts  15.6 us (5%)
  between operations  13.5 us (4%)
    psum x1, waiting for transfers between devices, local(): summed = lax.psum(total, 'tp')  96.1 us
    all_gather x1, waiting for transfers between devices, local(): lax.all_gather(output_weight, 'ep', axis=0, tiled=True)  52.5 us
    all_to_all x1, waiting for transfers between devices, local(): lax.all_to_all(outgoing, 'ep', split_axis=0, concat_axis=0, tiled=True)  52.2 us
    all_gather x1, waiting for transfers between devices, local(): lax.all_gather(query_weight, 'ep', axis=0, tiled=True)  21.8 us
    ppermute x1, waiting for transfers between devices, from_partner(): return lax.ppermute(value, axis, pairs)  18.4 us
    all_to_all x1, starting transfers between devices, local(): lax.all_to_all(outgoing, 'ep', split_axis=0, concat_axis=0, tiled=True)  9.71 us
    dot_general x1, matrix products, local(): jnp.einsum('ack,kf->acf', arrived, gate_up_weight[0], preferred_element_t...  7.91 us
  transfers between devices with their start and end apart: 7, of which 5 were waited for; matrix products, arithmetic and copies ran while one was open for 15% of the time, Pallas kernels for 0%

commit v1 on v0

v1 whole, which is shorter than its diff:
```python
import functools

import jax
import jax.numpy as jnp
from jax import lax
from jax.experimental import pallas as pl
from jax.experimental.pallas import tpu as pltpu
from jax.sharding import PartitionSpec as P

HD = 128
QH = 32
KVH = 4
TOPK = 8
SLOTS = 16

EPS = 1e-06
ROPE_BASE = 1000000.0
F32 = jnp.float32
BF16 = jnp.bfloat16
NT = (((1,), (1,)), ((), ()))
VMEM_LIMIT = 48 * 1024 * 1024


def vmem():
    return pl.BlockSpec(memory_space=pltpu.VMEM)


def smem():
    return pl.BlockSpec(memory_space=pltpu.SMEM)


def call(body, out_shape, args, flops, extra_bytes=0, scratch=(), specs=None, out_specs=None):
    moved = sum(a.size * a.dtype.itemsize for a in args)
    moved += sum(o.size * o.dtype.itemsize for o in out_shape)
    return pl.pallas_call(
        body,
        out_shape=out_shape,
        in_specs=specs or [smem()] + [vmem()] * (len(args) - 1),
        out_specs=out_specs or [vmem()] * len(out_shape),
        scratch_shapes=list(scratch),
        compiler_params=pltpu.CompilerParams(vmem_limit_bytes=VMEM_LIMIT),
        cost_estimate=pl.CostEstimate(
            flops=flops, bytes_accessed=moved + extra_bytes, transcendentals=0
        ),
    )(*args)


def inverse_rms(wide):
    return lax.rsqrt(jnp.mean(wide * wide, -1, keepdims=True) + EPS)


def slots_of(ids_ref, experts):
    rows = ids_ref.shape[0]
    ids = ids_ref[...]
    lane = lax.broadcasted_iota(jnp.int32, (rows, experts), 1)
    hit = ids[:, 0:1] == lane
    for k in range(1, TOPK):
        hit = hit | (ids[:, k : k + 1] == lane)
    below = lax.broadcasted_iota(jnp.int32, (rows, rows), 0)
    above = lax.broadcasted_iota(jnp.int32, (rows, rows), 1)
    lower = jnp.where(below > above, 1.0, 0.0).astype(BF16)
    earlier = jnp.dot(lower, jnp.where(hit, 1.0, 0.0).astype(BF16), preferred_element_type=F32)
    return hit, jnp.where(hit, earlier, -1.0).astype(BF16)


def dispatch_body(rank_ref, rows_ref, gain_ref, ids_ref, out_ref):
    rank = rank_ref[0]
    group, side = rank // 2, rank % 2
    width = out_ref.shape[1]
    places = out_ref.shape[0]
    experts = places // SLOTS * 4
    _, slot = slots_of(ids_ref, experts)
    place = lax.broadcasted_iota(jnp.int32, (places, experts), 0)
    expert = lax.broadcasted_iota(jnp.int32, (places, experts), 1)
    pick = jnp.where(expert == place // SLOTS * 4 + group, 1.0, 0.0).astype(BF16)
    spread = lax.dot_general(pick, slot, NT, preferred_element_type=F32)
    wanted = lax.broadcasted_iota(jnp.int32, spread.shape, 0) % SLOTS
    chosen = jnp.where(spread == wanted.astype(F32), 1.0, 0.0).astype(BF16)
    scale = inverse_rms(rows_ref[...].astype(F32))
    start = pl.multiple_of(side * width, width)
    half = rows_ref[:, pl.ds(start, width)].astype(F32)
    normed = (half * scale * gain_ref[:, pl.ds(start, width)]).astype(BF16)
    out_ref[...] = jnp.dot(chosen, normed, preferred_element_type=F32).astype(BF16)


def combine_map_body(rank_ref, rows_ref, gain_ref, router_ref, ids_ref, out_ref):
    group = rank_ref[0] // 2
    places = out_ref.shape[1]
    experts = router_ref.shape[0]
    hit, slot = slots_of(ids_ref, experts)
    wide = rows_ref[...].astype(F32)
    normed = (wide * inverse_rms(wide) * gain_ref[...]).astype(BF16)
    logits = lax.dot_general(normed, router_ref[...], NT, preferred_element_type=F32)
    scores = jnp.where(hit, jax.nn.sigmoid(logits), 0.0)
    gates = (scores / jnp.sum(scores, -1, keepdims=True)).astype(BF16)
    expert = lax.broadcasted_iota(jnp.int32, (experts, places), 0)
    place = lax.broadcasted_iota(jnp.int32, (experts, places), 1)
    pick = jnp.where(expert == place // SLOTS * 4 + group, 1.0, 0.0).astype(BF16)
    spread = jnp.dot(slot, pick, preferred_element_type=F32)
    gate = jnp.dot(gates, pick, preferred_element_type=F32)
    wanted = lax.broadcasted_iota(jnp.int32, spread.shape, 1) % SLOTS
    out_ref[...] = jnp.where(spread == wanted.astype(F32), gate, 0.0).astype(BF16)


def first_half_body(rank_ref, x_ref, w_ref, out_ref):
    out_ref[...] = jnp.dot(x_ref[...], w_ref[0], preferred_element_type=F32)


def expert_body(rank_ref, acc_ref, x_ref, w_ref, down_ref, kept_ref, handed_ref):
    side = rank_ref[0] % 2
    paired = acc_ref[...] + jnp.dot(x_ref[...], w_ref[0], preferred_element_type=F32)
    ff = paired.shape[1] // 2
    hidden = (jax.nn.silu(paired[:, :ff]) * paired[:, ff:]).astype(BF16)
    width = kept_ref.shape[1]
    mine = pl.multiple_of(side * width, width)
    other = pl.multiple_of((1 - side) * width, width)
    handed_ref[...] = jnp.dot(
        hidden, down_ref[0, :, pl.ds(other, width)], preferred_element_type=F32
    ).astype(BF16)
    kept_ref[...] = jnp.dot(
        hidden, down_ref[0, :, pl.ds(mine, width)], preferred_element_type=F32
    )


def attention_body(
    rank_ref, rows_ref, gain_ref, w_ref, qg_ref, kg_ref, cos_ref, sin_ref, kept_ref, handed_ref
):
    side = rank_ref[0] % 2
    seq = rows_ref.shape[0]
    heads = (w_ref.shape[1] // HD - 2) // 2
    wide = rows_ref[...].astype(F32)
    normed = (wide * inverse_rms(wide) * gain_ref[...]).astype(BF16)
    columns = (heads + 2) * HD
    qkv = jnp.dot(normed, w_ref[:, :columns], preferred_element_type=F32)
    cosine, sine = cos_ref[...], sin_ref[...]

    def turned(values, gain):
        values = values * inverse_rms(values) * gain
        return (values * cosine + pltpu.roll(values, HD // 2, 1) * sine).astype(BF16)

    keys = turned(qkv[:, heads * HD : (heads + 1) * HD], kg_ref[...])
    values = qkv[:, (heads + 1) * HD :].astype(BF16)
    below = lax.broadcasted_iota(jnp.int32, (seq, seq), 0)
    above = lax.broadcasted_iota(jnp.int32, (seq, seq), 1)
    causal = below >= above
    parts = []
    for head in range(heads):
        query = turned(qkv[:, head * HD : (head + 1) * HD], qg_ref[...])
        logits = lax.dot_general(query, keys, NT, preferred_element_type=F32) * HD**-0.5
        logits = jnp.where(causal, logits, -1e30)
        expo = jnp.exp(logits - jnp.max(logits, -1, keepdims=True))
        probs = (expo / jnp.sum(expo, -1, keepdims=True)).astype(BF16)
        parts.append(jnp.dot(probs, values, preferred_element_type=F32).astype(BF16))
    attended = jnp.concatenate(parts, 1)
    width = kept_ref.shape[1]
    mine = pl.multiple_of(side * width, width)
    other = pl.multiple_of((1 - side) * width, width)
    handed_ref[...] = lax.dot_general(
        attended, w_ref[pl.ds(other, width), columns:], NT, preferred_element_type=F32
    ).astype(BF16)
    kept_ref[...] = lax.dot_general(
        attended, w_ref[pl.ds(mine, width), columns:], NT, preferred_element_type=F32
    )


def combine_body(map_ref, back_ref, kept_ref, got_ref, out_ref):
    total = jnp.dot(map_ref[...], back_ref[...], preferred_element_type=F32)
    out_ref[...] = (total + kept_ref[...] + got_ref[...].astype(F32)).astype(BF16)


def local(
    residual_in,
    shortcut,
    attn_gain,
    moe_gain,
    query_weight,
    key_value,
    output_weight,
    query_gain,
    key_gain,
    router_weight,
    expert_ids,
    gate_up_weight,
    down_weight,
):
    n_ep = lax.axis_size("ep")
    n_tp = lax.axis_size("tp")
    rank = lax.axis_index("tp")
    ranks = rank.astype(jnp.int32)[None]
    side = rank % 2
    group_id = rank // 2
    pairs = n_tp // 2
    rows, d_model = residual_in.shape
    half = d_model // 2
    places = n_ep * SLOTS
    ff2 = gate_up_weight.shape[2]
    ff = ff2 // 2
    qh_dev = query_weight.shape[1] // HD
    kv_head = rank * qh_dev // (QH // KVH)
    partner = [(i, i ^ 1) for i in range(n_tp)]
    sides = [[2 * i + h for i in range(pairs)] for h in range(2)]

    own_key = lax.dynamic_slice_in_dim(key_value, kv_head * HD, HD, 1)
    own_value = lax.dynamic_slice_in_dim(key_value, (KVH + kv_head) * HD, HD, 1)
    packed = jnp.concatenate([query_weight, own_key, own_value, output_weight], 1)
    weights = lax.all_gather(packed, "ep", axis=0, tiled=True)

    moe_gain = moe_gain[None, :]
    (outgoing,) = call(
        dispatch_body,
        [jax.ShapeDtypeStruct((places, half), BF16)],
        (ranks, shortcut, moe_gain, expert_ids),
        2 * places * rows * half,
    )
    arrived = lax.all_to_all(outgoing, "ep", split_axis=0, concat_axis=0, tiled=True)
    (combine,) = call(
        combine_map_body,
        [jax.ShapeDtypeStruct((rows, places), BF16)],
        (ranks, shortcut, moe_gain, router_weight, expert_ids),
        2 * rows * 128 * d_model,
    )
    received = lax.ppermute(arrived, "tp", partner)

    def chosen_half(which):
        return pl.BlockSpec((1, half, ff2), lambda i, rank_ref: (0, which(rank_ref[0] % 2), 0))

    def whole(shape):
        return pl.BlockSpec(shape, lambda i, rank_ref: (0,) * len(shape))

    (acc,) = pl.pallas_call(
        first_half_body,
        out_shape=[jax.ShapeDtypeStruct((places, ff2), F32)],
        grid_spec=pltpu.PrefetchScalarGridSpec(
            num_scalar_prefetch=1,
            grid=(1,),
            in_specs=[whole((places, half)), chosen_half(lambda s: s)],
            out_specs=[whole((places, ff2))],
        ),
        compiler_params=pltpu.CompilerParams(vmem_limit_bytes=VMEM_LIMIT),
        cost_estimate=pl.CostEstimate(
            flops=2 * places * half * ff2, bytes_accessed=half * ff2 * 2 + places * ff2 * 4, transcendentals=0
        ),
    )(ranks, arrived, gate_up_weight)
    kept, handed = pl.pallas_call(
        expert_body,
        out_shape=[
            jax.ShapeDtypeStruct((places, half), F32),
            jax.ShapeDtypeStruct((places, half), BF16),
        ],
        grid_spec=pltpu.PrefetchScalarGridSpec(
            num_scalar_prefetch=1,
            grid=(1,),
            in_specs=[
                whole((places, ff2)),
                whole((places, half)),
                chosen_half(lambda s: 1 - s),
                whole((1, ff, d_model)),
            ],
            out_specs=[whole((places, half)), whole((places, half))],
        ),
        compiler_params=pltpu.CompilerParams(vmem_limit_bytes=VMEM_LIMIT),
        cost_estimate=pl.CostEstimate(
            flops=2 * places * half * ff2 + 2 * places * ff * d_model,
            bytes_accessed=half * ff2 * 2 + places * ff2 * 4 + ff * d_model * 2,
            transcendentals=0,
        ),
    )(ranks, acc, received, gate_up_weight, down_weight)
    got = lax.ppermute(handed, "tp", partner)
    expert_out = (kept + got.astype(F32)).astype(BF16)
    returned = lax.all_to_all(expert_out, "ep", split_axis=0, concat_axis=0, tiled=True)

    position = jnp.arange(rows, dtype=F32)
    freq = ROPE_BASE ** (-jnp.arange(HD // 2, dtype=F32) * 2.0 / HD)
    angle = position[:, None] * freq[None, :]
    cosine, sine = jnp.cos(angle), jnp.sin(angle)
    cosine = jnp.concatenate([cosine, cosine], 1)
    sine = jnp.concatenate([-sine, sine], 1)
    att_kept, att_handed = call(
        attention_body,
        [jax.ShapeDtypeStruct((rows, half), F32), jax.ShapeDtypeStruct((rows, half), BF16)],
        (
            ranks,
            residual_in,
            attn_gain[None, :],
            weights,
            query_gain[None, :],
            key_gain[None, :],
            cosine,
            sine,
        ),
        2 * rows * d_model * weights.shape[1],
    )
    att_got = lax.ppermute(att_handed, "tp", partner)
    (total,) = call(
        combine_body,
        [jax.ShapeDtypeStruct((rows, half), BF16)],
        (combine, returned, att_kept, att_got),
        2 * rows * places * half,
        specs=[vmem()] * 4,
    )
    terms = lax.all_to_all(
        total.reshape(pairs, rows // pairs, half),
        "tp",
        split_axis=0,
        concat_axis=0,
        tiled=True,
        axis_index_groups=sides,
    )
    share = rows // pairs
    own = lax.dynamic_slice(residual_in, (group_id * share, side * half), (share, half))
    mine = (own.astype(F32) + jnp.sum(terms.astype(F32), 0)).astype(BF16)
    everyone = lax.all_to_all(
        jnp.broadcast_to(mine[None], (n_tp, share, half)), "tp", split_axis=0, concat_axis=0, tiled=True
    )
    return everyone.reshape(pairs, 2, share, half).transpose(0, 2, 1, 3).reshape(rows, d_model)


def solution(mesh):
    return jax.shard_map(
        local,
        mesh=mesh,
        in_specs=(
            P("ep", None),
            P("ep", None),
            P(),
            P(),
            P("ep", "tp"),
            P("ep", None),
            P("ep", "tp"),
            P(),
            P(),
            P(),
            P("ep", None),
            P(("ep", "tp"), None, None),
            P(("ep", "tp"), None, None),
        ),
        out_specs=P("ep", None),
        check_vma=False,
    )
```

time: 332 us -> 196 us (0.59)
  waiting for transfers between devices: 242 us -> 62.3 us
  blocking collectives: 0 us -> 63.4 us
  matrix products: 26.4 us -> 0 us
  Pallas kernels: 0 us -> 21.8 us
  other arithmetic: 17.7 us -> 4.18 us
  local copies, waits for them, and re-layouts: 15.6 us -> 10.6 us
  starting transfers between devices: 15.9 us -> 19.4 us
    psum x1 -> x0, waiting for transfers between devices: 96.1 us -> none  [local(): summed = lax.psum(total, 'tp')]
    all_gather x3 -> x1, waiting for transfers between devices: 74.3 us -> 0.01 us  [local(): weights = lax.all_gather(packed, 'ep', axis=0, tiled=True)]
    all_to_all x0 -> x2, blocking collectives: none -> 63.4 us  [the longest x1 47.9 us: local(): lax.all_to_all(outgoing, 'ep', split_axis=0, concat_axis=0, tiled=True)]
    all_to_all x1, waiting for transfers between devices: 52.2 us -> 8.73 us  [local(): lax.all_to_all(total.reshape(pairs, rows // pairs, half), 'tp', split_axi...]
    dot_general x11 -> x0, matrix products: 26.4 us -> none  [the longest x1 7.91 us: local(): jnp.einsum('ack,kf->acf', arrived, gate_up_weight[0], preferred_element_t...]
    pallas_call x0 -> x6, Pallas kernels: none -> 21.8 us  [the longest x4 10.8 us: call(): pl.pallas_call(body, out_shape=out_shape, in_specs=specs or [smem()] + [v...]
    ppermute x1 -> x3, waiting for transfers between devices: 18.4 us -> 37.4 us  [the longest x1 21 us: local(): got = lax.ppermute(handed, 'tp', partner)]
    all_to_all x1, waiting for transfers between devices: 0.01 us -> 16.1 us  [local(): lax.all_to_all(expert_out, 'ep', split_axis=0, concat_axis=0, tiled=True)]
  transfers between devices with their start and end apart: 7 -> 6, of which waited for: 5 -> 4; matrix products, arithmetic and copies ran while one was open for 15% -> 2% of each run, Pallas kernels for 0% -> 10%
where the time goes in v1:
time: 196 us; the launch traced here: 195 us
  blocking collectives  63.4 us (32%)
  waiting for transfers between devices  62.3 us (32%)
  Pallas kernels  21.8 us (11%)
  starting transfers between devices  19.4 us (10%)
  between operations  13.5 us (7%)
  local copies, waits for them, and re-layouts  10.6 us (5%)
  other arithmetic  4.18 us (2%)
    all_to_all x1, blocking collectives, local(): lax.all_to_all(outgoing, 'ep', split_axis=0, concat_axis=0, tiled=True)  47.9 us
    ppermute x1, waiting for transfers between devices, local(): got = lax.ppermute(handed, 'tp', partner)  21 us
    ppermute x1, waiting for transfers between devices, local(): received = lax.ppermute(arrived, 'tp', partner)  16.4 us
    all_to_all x1, waiting for transfers between devices, local(): lax.all_to_all(expert_out, 'ep', split_axis=0, concat_axis=0, tiled=True)  16.1 us
    all_to_all x1, blocking collectives, local(): lax.all_to_all(jnp.broadcast_to(mine[None], (n_tp, share, half)), 'tp', s...  15.4 us
    pallas_call x4, Pallas kernels, call(): pl.pallas_call(body, out_shape=out_shape, in_specs=specs or [smem()] + [v...  10.8 us
    unnamed x30, local copies, waits for them, and re-layouts  8.94 us
    all_to_all x1, waiting for transfers between devices, local(): lax.all_to_all(total.reshape(pairs, rows // pairs, half), 'tp', split_axi...  8.73 us
  transfers between devices with their start and end apart: 6, of which 4 were waited for; matrix products, arithmetic and copies ran while one was open for 2% of the time, Pallas kernels for 10%

profile of v1, /device:TPU:32, one launch (start us, length us, event | category | flops | bytes accessed | tf_op | source)
XLA Modules:
  0.0 195.1 jit_solution(15300187406666211236)
XLA Ops:
  6.5 0.0 all-gather.2.cloned.1.call-start
  6.5 0.7 constant_dynamic-slice_fusion.1
  7.3 1.6 pad_maximum_fusion
  8.8 0.0 all-gather.2.cloned.1.call-update
  8.9 0.8 copy.18.ids_ref
  9.7 0.0 copy-start.1
  9.7 1.1 copy-done.1
  10.8 0.7 copy-done.9
  11.5 1.1 shard_map.128
  12.6 47.9 %all_to_all.32 = bf16[32,16,1024]{2,1,0:T(8,128)(2,1)S(1)} all-to-all(bf16[32,16,1024]{2,1,0:T(8,128)(2,1)S(1)} %bitcast.16), channel_id=1, replica_groups=mesh['ep'=32,'tp'=8] {'ep'}, dimensions={0} | all-to-all | bytes 2097152 | tf_op jit(solution)/shard_map/all_to_all | solution.py:215
  60.6 1.6 collective-permute-start
  62.2 3.7 %shard_map.129.acc_ref = f32[512,1536]{1,0:T(8,128)S(1)} custom-call(s32[1]{0:T(128)} %bitcast.rank_ref, bf16[512,1024]{1,0:T(8,128)(2,1)S(1)} %bitcast.19, bf16[1,2048,1536]{2,1,0:T(8,128)(2,1)} %w_ref.3), custom_call_target="tpu_custom_call" | custom-call | flops 1610612736 | bytes 6291456 | tf_op jit(solution)/shard_map/pallas_call | solution.py:230
  65.9 0.0 copy-start
  65.9 1.7 copy-done
  67.6 16.4 %collective-permute-done.x_ref = bf16[512,1024]{1,0:T(8,128)(2,1)S(1)} collective-permute-done((bf16[512,1024]{1,0:T(8,128)(2,1)S(1)}, bf16[512,1024]{1,0:T(8,128)(2,1)S(1)}, u32[]{:S(2)}, u32[]{:S(2)}) %collective-permute-start) | collective-permute-done | bytes 1048608 | tf_op jit(solution)/shard_map/ppermute | solution.py:222
  84.0 7.3 %shard_map.130 = (f32[512,1024]{1,0:T(8,128)S(1)}, bf16[512,1024]{1,0:T(8,128)(2,1)S(1)}) custom-call(s32[1]{0:T(128)} %bitcast.rank_ref, f32[512,1536]{1,0:T(8,128)} %copy-done, bf16[512,1024]{1,0:T(8,128)(2,1)S(1)} %collective-permute-done.x_ref, bf16[1,2048,1536]{2,1,0:T(8,128)(2,1)} %w_ref.3, bf16[1,768,2048]{2,1,0:T(8,128)(2,1)} %down_ref.1), custom_call_target="tpu_custom_call" | custom-call | flops 3221225472 | bytes 9437184 | tf_op jit(solution)/shard_map/pallas_call | solution.py:244
  91.3 1.7 collective-permute-start.1
  93.0 21.0 %collective-permute-done.1 = bf16[512,1024]{1,0:T(8,128)(2,1)S(1)} collective-permute-done((bf16[512,1024]{1,0:T(8,128)(2,1)S(1)}, bf16[512,1024]{1,0:T(8,128)(2,1)S(1)}, u32[]{:S(2)}, u32[]{:S(2)}) %collective-permute-start.1) | collective-permute-done | bytes 1048608 | tf_op jit(solution)/shard_map/ppermute | solution.py:268
  114.0 1.3 add_convert_fusion
  115.4 8.3 %all-to-all-start.1 = ((bf16[32,16,1024]{2,1,0:T(8,128)(2,1)}), bf16[32,16,1024]{2,1,0:T(8,128)(2,1)S(1)}, u32[]{:S(2)}, u32[]{:S(2)}) async-start(bf16[32,16,1024]{2,1,0:T(8,128)(2,1)} %bitcast.4), calls=%async_computation.1 | async-start | bytes 2097152 | tf_op jit(solution)/shard_map/all_to_all | solution.py:270
  123.7 0.4 fusion.2
  124.0 0.0 copy-start.10
  124.1 0.8 pad_maximum_fusion.1
  124.9 0.0 copy-done.3
  124.9 0.0 copy-done.11
  124.9 0.0 copy-done.12
  124.9 0.0 copy-done.13
  124.9 0.0 copy-start.7
  124.9 1.0 copy-done.7
  125.9 0.9 copy-done.8
  126.8 6.5 %shard_map.131 = (f32[192,1024]{1,0:T(8,128)S(1)}, bf16[192,1024]{1,0:T(8,128)(2,1)}) custom-call(s32[1]{0:T(128)} %bitcast.rank_ref, bf16[192,2048]{1,0:T(8,128)(2,1)S(1)} %copy-done.3, f32[1,2048]{1,0:T(1,128)S(1)} %bitcast.22, bf16[2048,1280]{1,0:T(8,128)(2,1)} %all-gather.2.cloned.1.call-done.w_ref, f32[1,128]{1,0:T(1,128)S(1)} %bitcast.23, ...), custom_call_target="tpu_custom_call" | custom-call | flops 1006632960 | bytes 7414788 | tf_op jit(solution)/shard_map/pallas_call | solution.py:35
  133.3 1.5 collective-permute-start.2
  134.7 0.0 copy-done.10
  134.7 0.0 copy-done.2
  134.7 0.0 copy-done.6
  134.7 1.1 shard_map.127.map_ref
  135.9 0.7 copy-done.4
  136.5 16.1 %all-to-all-done.1 = bf16[32,16,1024]{2,1,0:T(8,128)(2,1)S(1)} async-done(((bf16[32,16,1024]{2,1,0:T(8,128)(2,1)}), bf16[32,16,1024]{2,1,0:T(8,128)(2,1)S(1)}, u32[]{:S(2)}, u32[]{:S(2)}) %all-to-all-start.1) | async-done | bytes 1048608 | tf_op jit(solution)/shard_map/all_to_all | solution.py:270
  152.6 0.0 collective-permute-done.2.got_ref
  152.6 0.9 copy-done.5
  153.6 2.1 %shard_map.132 = bf16[192,1024]{1,0:T(8,128)(2,1)} custom-call(bf16[192,512]{1,0:T(8,128)(2,1)S(1)} %copy-done.5, bf16[512,1024]{1,0:T(8,128)(2,1)S(1)} %bitcast.17, f32[192,1024]{1,0:T(8,128)S(1)} %get-tuple-element.11.kept_ref, bf16[192,1024]{1,0:T(8,128)(2,1)} %collective-permute-done.2.got_ref), custom_call_target="tpu_custom_call" | custom-call | flops 201326592 | bytes 2818048 | tf_op jit(solution)/shard_map/pallas_call | solution.py:35
  155.7 6.3 %all-to-all-start.2 = ((bf16[4,48,1024]{2,1,0:T(8,128)(2,1)}), bf16[4,48,1024]{2,1,0:T(8,128)(2,1)S(1)}, u32[]{:S(2)}, u32[]{:S(2)}) async-start(bf16[4,48,1024]{2,1,0:T(8,128)(2,1)} %bitcast.9), calls=%async_computation.2 | async-start | bytes 786432 | tf_op jit(solution)/shard_map/all_to_all | solution.py:301
  162.0 8.7 %all-to-all-done.2 = bf16[4,48,1024]{2,1,0:T(8,128)(2,1)S(1)} async-done(((bf16[4,48,1024]{2,1,0:T(8,128)(2,1)}), bf16[4,48,1024]{2,1,0:T(8,128)(2,1)S(1)}, u32[]{:S(2)}, u32[]{:S(2)}) %all-to-all-start.2) | async-done | bytes 393248 | tf_op jit(solution)/shard_map/all_to_all | solution.py:301
  170.8 0.1 convert_reduce_fusion
  170.9 0.1 broadcast_in_dim.28
  171.0 15.4 %all_to_all.33 = bf16[8,48,1024]{2,1,0:T(8,128)(2,1)S(1)} all-to-all(bf16[8,48,1024]{2,1,0:T(8,128)(2,1)S(1)} %broadcast_in_dim.28), channel_id=1, replica_groups=mesh['ep'=32,'tp'=8] {'tp'}, dimensions={0} | all-to-all | bytes 1572864 | tf_op jit(solution)/shard_map/all_to_all | solution.py:312
  186.4 0.8 copy.20
  187.2 1.1 copy.21
  (13 shorter events, 0.1 us)
Async XLA Ops:
  6.5 118.3 %all-gather.2.cloned.1.call-start = ((), (), s32[]{:S(2)}) async-start(), calls=%async_computation.4 | async-start | bytes 5406720 | tf_op jit(solution)/shard_map/all_gather | solution.py:206
  9.7 1.1 copy-start.1
  10.8 0.7 copy-start.9
  60.6 23.5 %collective-permute-start = (bf16[512,1024]{1,0:T(8,128)(2,1)S(1)}, bf16[512,1024]{1,0:T(8,128)(2,1)S(1)}, u32[]{:S(2)}, u32[]{:S(2)}) collective-permute-start(bf16[512,1024]{1,0:T(8,128)(2,1)S(1)} %bitcast.18), channel_id=1, source_target_pairs={{0,1},{1,0},{2,3},{3,2},{4,5},{5,4},{6,7},{7,6},{8,9},{9,8},{10,11... | collective-permute-start | bytes 3145736 | tf_op jit(solution)/shard_map/ppermute | solution.py:222
  65.9 1.7 copy-start
  91.3 22.7 %collective-permute-start.1 = (bf16[512,1024]{1,0:T(8,128)(2,1)S(1)}, bf16[512,1024]{1,0:T(8,128)(2,1)S(1)}, u32[]{:S(2)}, u32[]{:S(2)}) collective-permute-start(bf16[512,1024]{1,0:T(8,128)(2,1)S(1)} %get-tuple-element.10), channel_id=1, source_target_pairs={{0,1},{1,0},{2,3},{3,2},{4,5},{5,4},{6,7},{7,6},{8,9},{9,8},{10,11... | collective-permute-start | bytes 3145736 | tf_op jit(solution)/shard_map/ppermute | solution.py:268
  114.0 10.9 %copy-start.3 = (bf16[192,2048]{1,0:T(8,128)(2,1)S(1)}, bf16[192,2048]{1,0:T(8,128)(2,1)}, u32[]{:S(2)}) copy-start(bf16[192,2048]{1,0:T(8,128)(2,1)} %rows_ref.5) | copy-start | bytes 2359300
  114.0 10.9 %copy-start.11 = (f32[2048]{0:T(1024)S(1)}, f32[2048]{0:T(1024)}, u32[]{:S(2)}) copy-start(f32[2048]{0:T(1024)} %param.15) | copy-start | bytes 24580
  114.0 10.9 %copy-start.12 = (f32[128]{0:T(128)S(1)}, f32[128]{0:T(128)}, u32[]{:S(2)}) copy-start(f32[128]{0:T(128)} %param.20) | copy-start | bytes 1540
  114.0 10.9 %copy-start.13 = (f32[128]{0:T(128)S(1)}, f32[128]{0:T(128)}, u32[]{:S(2)}) copy-start(f32[128]{0:T(128)} %param.21) | copy-start | bytes 1540
  115.4 37.3 %all-to-all-start.1 = ((bf16[32,16,1024]{2,1,0:T(8,128)(2,1)}), bf16[32,16,1024]{2,1,0:T(8,128)(2,1)S(1)}, u32[]{:S(2)}, u32[]{:S(2)}) async-start(bf16[32,16,1024]{2,1,0:T(8,128)(2,1)} %bitcast.4), calls=%async_computation.1 | async-start | bytes 2097152 | tf_op jit(solution)/shard_map/all_to_all | solution.py:270
  124.0 10.7 %copy-start.10 = (f32[2048]{0:T(1024)S(1)}, f32[2048]{0:T(1024)}, u32[]{:S(2)}) copy-start(f32[2048]{0:T(1024)} %param.16) | copy-start | bytes 24580
  124.9 9.9 %copy-start.2 = (bf16[192,2048]{1,0:T(8,128)(2,1)S(1)}, bf16[192,2048]{1,0:T(8,128)(2,1)}, u32[]{:S(2)}) copy-start(bf16[192,2048]{1,0:T(8,128)(2,1)} %rows_ref.4) | copy-start | bytes 2359300
  124.9 9.9 %copy-start.6 = (bf16[128,2048]{1,0:T(8,128)(2,1)S(1)}, bf16[128,2048]{1,0:T(8,128)(2,1)}, u32[]{:S(2)}) copy-start(bf16[128,2048]{1,0:T(8,128)(2,1)} %router_ref.1) | copy-start | bytes 1572868
  124.9 1.0 copy-start.7
  125.9 0.9 copy-start.8
  133.3 19.4 %collective-permute-start.2 = (bf16[192,1024]{1,0:T(8,128)(2,1)}, bf16[192,1024]{1,0:T(8,128)(2,1)}, u32[]{:S(2)}, u32[]{:S(2)}) collective-permute-start(bf16[192,1024]{1,0:T(8,128)(2,1)} %get-tuple-element.12), channel_id=1, source_target_pairs={{0,1},{1,0},{2,3},{3,2},{4,5},{5,4},{6,7},{7,6},{8,9},{9,8},{10,11... | collective-permute-start | bytes 1179656 | tf_op jit(solution)/shard_map/ppermute | solution.py:293
  135.8 0.7 copy-start.4
  152.6 0.9 copy-start.5
  155.7 15.1 %all-to-all-start.2 = ((bf16[4,48,1024]{2,1,0:T(8,128)(2,1)}), bf16[4,48,1024]{2,1,0:T(8,128)(2,1)S(1)}, u32[]{:S(2)}, u32[]{:S(2)}) async-start(bf16[4,48,1024]{2,1,0:T(8,128)(2,1)} %bitcast.9), calls=%async_computation.2 | async-start | bytes 786432 | tf_op jit(solution)/shard_map/all_to_all | solution.py:301
Sparse Core Ops, SparseCore 0:
  9.2 83.3 all-gather.1

commit v2 on v1

v2 whole, which is shorter than its diff:
```python
import functools

import jax
import jax.numpy as jnp
from jax import lax
from jax.experimental import pallas as pl
from jax.experimental.pallas import tpu as pltpu
from jax.sharding import PartitionSpec as P

HD = 128
QH = 32
KVH = 4
TOPK = 8
SLOTS = 16

EPS = 1e-06
ROPE_BASE = 1000000.0
F32 = jnp.float32
BF16 = jnp.bfloat16
NT = (((1,), (1,)), ((), ()))
VMEM_LIMIT = 56 * 1024 * 1024


def vmem():
    return pl.BlockSpec(memory_space=pltpu.VMEM)


def anywhere():
    return pl.BlockSpec(memory_space=pl.ANY)


def call(body, out_shape, args, flops, extra_bytes=0, scratch=(), specs=None, out_specs=None, aliases=None, cost=None):
    moved = extra_bytes + sum(a.size * a.dtype.itemsize for a in args)
    moved += sum(o.size * o.dtype.itemsize for o in out_shape)
    return pl.pallas_call(
        body,
        out_shape=out_shape,
        in_specs=specs or [vmem()] * len(args),
        out_specs=out_specs or [vmem()] * len(out_shape),
        scratch_shapes=list(scratch),
        input_output_aliases=aliases or {},
        compiler_params=pltpu.CompilerParams(vmem_limit_bytes=VMEM_LIMIT),
        cost_estimate=pl.CostEstimate(
            flops=flops if cost is None else cost,
            bytes_accessed=moved if cost is None else cost,
            transcendentals=0,
        ),
    )(*args)


def inverse_rms(wide):
    return lax.rsqrt(jnp.mean(wide * wide, -1, keepdims=True) + EPS)


def slots_of(ids_ref, experts):
    rows = ids_ref.shape[1]
    expert = lax.broadcasted_iota(jnp.int32, (experts, rows), 0)
    hit = ids_ref[0:1, :] == expert
    for k in range(1, TOPK):
        hit = hit | (ids_ref[k : k + 1, :] == expert)
    before = lax.broadcasted_iota(jnp.int32, (rows, rows), 0)
    after = lax.broadcasted_iota(jnp.int32, (rows, rows), 1)
    upper = jnp.where(before < after, 1.0, 0.0).astype(BF16)
    earlier = jnp.dot(jnp.where(hit, 1.0, 0.0).astype(BF16), upper, preferred_element_type=F32)
    slot = jnp.where(hit, earlier, -1.0).astype(BF16)
    places = experts // 4 * SLOTS
    place = lax.broadcasted_iota(jnp.int32, (places, experts), 0)
    column = lax.broadcasted_iota(jnp.int32, (places, experts), 1)
    group = lax.axis_index("tp") // 2
    pick = jnp.where(column == place // SLOTS * 4 + group, 1.0, 0.0).astype(BF16)
    spread = jnp.dot(pick, slot, preferred_element_type=F32)
    wanted = lax.broadcasted_iota(jnp.int32, spread.shape, 0) % SLOTS
    return hit, pick, spread == wanted.astype(F32)


def dispatch_body(rows_ref, gain_ref, ids_ref, shared_ref, direct_ref):
    side = lax.axis_index("tp") % 2
    places, width = shared_ref.shape
    _, _, filled = slots_of(ids_ref, places // SLOTS * 4)
    chosen = jnp.where(filled, 1.0, 0.0).astype(BF16)
    scale = inverse_rms(rows_ref[...].astype(F32))

    def place_columns(columns, out_ref):
        part = rows_ref[:, columns].astype(F32)
        normed = (part * scale * gain_ref[:, columns]).astype(BF16)
        out_ref[...] = jnp.dot(chosen, normed, preferred_element_type=F32).astype(BF16)

    place_columns(pl.ds(pl.multiple_of(side * width, width), width), shared_ref)
    place_columns(pl.ds(2 * width, direct_ref.shape[1]), direct_ref)


def combine_map_body(rows_ref, gain_ref, router_ref, ids_ref, out_ref):
    hit, pick, filled = slots_of(ids_ref, router_ref.shape[0])
    wide = rows_ref[...].astype(F32)
    normed = (wide * inverse_rms(wide) * gain_ref[...]).astype(BF16)
    logits = lax.dot_general(router_ref[...], normed, NT, preferred_element_type=F32)
    scores = jnp.where(hit, jax.nn.sigmoid(logits), 0.0)
    gates = (scores / jnp.sum(scores, 0, keepdims=True)).astype(BF16)
    gate = jnp.dot(pick, gates, preferred_element_type=F32)
    out_ref[...] = jnp.where(filled, gate, 0.0).T.astype(BF16)


def relay_body(value_ref, after_ref, out_ref):
    pass


def first_part_body(own_ref, w_ref, out_ref, w_buf, sem):
    width = own_ref.shape[1]
    mine = pl.multiple_of(lax.axis_index("tp") % 2 * width, width)
    copy = pltpu.make_async_copy(w_ref.at[0, pl.ds(mine, width)], w_buf, sem)
    copy.start()
    copy.wait()
    out_ref[...] = jnp.dot(own_ref[...], w_buf[...], preferred_element_type=F32)


def expert_body(
    acc_ref,
    got_ref,
    both_ref,
    w_ref,
    down_ref,
    near_ref,
    direct_ref,
    handed_ref,
    kept_ref,
    acc,
    x_buf,
    w_buf,
    w_down,
    hidden,
    out_direct,
    out_handed,
    out_kept,
    sems,
):
    side = lax.axis_index("tp") % 2
    width = out_kept.shape[1]
    mine = pl.multiple_of(side * width, width)
    other = pl.multiple_of((1 - side) * width, width)
    ff = hidden.shape[1]
    tile = 256
    moves = [
        (got_ref, x_buf.at[:, :width]),
        (both_ref, x_buf.at[:, width:]),
    ]
    for start in (0, ff):
        columns = pl.ds(start, ff)
        moves.append((w_ref.at[0, pl.ds(other, width), columns], w_buf.at[:width, columns]))
        moves.append((w_ref.at[0, 2 * width :, columns], w_buf.at[width:, columns]))
    moves.append((acc_ref, acc))
    moves.append((down_ref.at[0], w_down))
    copies = [pltpu.make_async_copy(a, b, sems.at[i]) for i, (a, b) in enumerate(moves)]
    for copy in copies:
        copy.start()
    for copy in copies[:-1]:
        copy.wait()
    x = x_buf[...]
    for at in range(0, ff, tile):
        gate = acc[:, at : at + tile] + jnp.dot(
            x, w_buf[:, at : at + tile], preferred_element_type=F32
        )
        up = acc[:, ff + at : ff + at + tile] + jnp.dot(
            x, w_buf[:, ff + at : ff + at + tile], preferred_element_type=F32
        )
        hidden[:, at : at + tile] = (jax.nn.silu(gate) * up).astype(BF16)
    copies[-1].wait()

    def projected(columns):
        return jnp.dot(hidden[...], w_down[:, columns], preferred_element_type=F32).astype(BF16)

    out_handed[...] = projected(pl.ds(other, width))
    back = [pltpu.make_async_copy(out_handed, handed_ref, sems.at[8])]
    back[0].start()
    out_direct[...] = projected(pl.ds(2 * width, out_direct.shape[1]))
    back.append(pltpu.make_async_copy(out_direct, direct_ref, sems.at[9]))
    back[1].start()
    out_kept[...] = projected(pl.ds(mine, width))
    back.append(pltpu.make_async_copy(out_kept, kept_ref, sems.at[10]))
    back[2].start()
    for copy in back:
        copy.wait()


def attention_body(
    rows_ref,
    gain_ref,
    near_ref,
    across_ref,
    other_near_ref,
    other_across_ref,
    qg_ref,
    kg_ref,
    cos_ref,
    sin_ref,
    handed_ref,
    kept_ref,
    direct_ref,
    w_ref,
):
    side = lax.axis_index("tp") % 2
    place = lax.axis_index("ep")
    along, core = place // 16, place % 2
    sources = (
        (near_ref, along, core),
        (across_ref, 1 - along, core),
        (other_near_ref, along, 1 - core),
        (other_across_ref, 1 - along, 1 - core),
    )
    block = w_ref.shape[0] // 32
    for ref, x_at, core_at in sources:
        for z in range(8):
            start = pl.multiple_of(((x_at * 8 + z) * 2 + core_at) * block, block)
            w_ref[pl.ds(start, block), :] = ref[z * block : (z + 1) * block, :]
    seq = rows_ref.shape[0]
    heads = (w_ref.shape[1] // HD - 2) // 2
    wide = rows_ref[...].astype(F32)
    normed = (wide * inverse_rms(wide) * gain_ref[...]).astype(BF16)
    columns = (heads + 2) * HD
    qkv = jnp.dot(normed, w_ref[:, :columns], preferred_element_type=F32)
    cosine, sine = cos_ref[...], sin_ref[...]

    def turned(values, gain):
        values = values * inverse_rms(values) * gain
        return (values * cosine + pltpu.roll(values, HD // 2, 1) * sine).astype(BF16)

    keys = turned(qkv[:, heads * HD : (heads + 1) * HD], kg_ref[...])
    values = qkv[:, (heads + 1) * HD :].astype(BF16)
    below = lax.broadcasted_iota(jnp.int32, (seq, seq), 0)
    above = lax.broadcasted_iota(jnp.int32, (seq, seq), 1)
    causal = below >= above
    parts = []
    for head in range(heads):
        query = turned(qkv[:, head * HD : (head + 1) * HD], qg_ref[...])
        logits = lax.dot_general(query, keys, NT, preferred_element_type=F32) * HD**-0.5
        logits = jnp.where(causal, logits, -1e30)
        expo = jnp.exp(logits - jnp.max(logits, -1, keepdims=True))
        probs = (expo / jnp.sum(expo, -1, keepdims=True)).astype(BF16)
        parts.append(jnp.dot(probs, values, preferred_element_type=F32).astype(BF16))
    attended = jnp.concatenate(parts, 1)
    width = kept_ref.shape[1]
    mine = pl.multiple_of(side * width, width)
    other = pl.multiple_of((1 - side) * width, width)
    handed_ref[...] = lax.dot_general(
        attended, w_ref[pl.ds(other, width), columns:], NT, preferred_element_type=F32
    ).astype(BF16)
    kept_ref[...] = lax.dot_general(
        attended, w_ref[pl.ds(mine, width), columns:], NT, preferred_element_type=F32
    )
    direct_ref[...] = lax.dot_general(
        attended, w_ref[2 * width :, columns:], NT, preferred_element_type=F32
    )


def combine_body(map_ref, shared_ref, both_ref, kept_ref, got_ref, direct_ref, out_ref):
    width = kept_ref.shape[1]
    shared = jnp.dot(map_ref[...], shared_ref[...], preferred_element_type=F32)
    out_ref[:, :width] = (shared + kept_ref[...] + got_ref[...].astype(F32)).astype(BF16)
    both = jnp.dot(map_ref[...], both_ref[...], preferred_element_type=F32)
    out_ref[:, width:] = (both + direct_ref[...]).astype(BF16)


def local(
    residual_in,
    shortcut,
    attn_gain,
    moe_gain,
    query_weight,
    key_value,
    output_weight,
    query_gain,
    key_gain,
    router_weight,
    expert_ids,
    gate_up_weight,
    down_weight,
):
    n_ep = lax.axis_size("ep")
    n_tp = lax.axis_size("tp")
    rank = lax.axis_index("tp")
    rows, d_model = residual_in.shape
    direct = d_model // 4
    shared = (d_model - direct) // 2
    places = n_ep * SLOTS
    ff2 = gate_up_weight.shape[2]
    ff = ff2 // 2
    qh_dev = query_weight.shape[1] // HD
    kv_head = rank * qh_dev // (QH // KVH)
    along_z = [[x * 16 + z * 2 + c for z in range(8)] for x in range(2) for c in range(2)]
    partner = [(i, i ^ 1) for i in range(n_tp)]

    own_key = lax.dynamic_slice_in_dim(key_value, kv_head * HD, HD, 1)
    own_value = lax.dynamic_slice_in_dim(key_value, (KVH + kv_head) * HD, HD, 1)
    packed = jnp.concatenate([query_weight, own_key, own_value, output_weight], 1)
    near = lax.all_gather(packed, "ep", axis=0, tiled=True, axis_index_groups=along_z)

    def to_owners(value):
        return lax.all_to_all(value, "ep", split_axis=0, concat_axis=0, tiled=True)

    def swapped(value):
        return lax.ppermute(value, "tp", partner)

    moe_gain = moe_gain[None, :]
    ids = expert_ids.T
    outgoing, outgoing_both = call(
        dispatch_body,
        [
            jax.ShapeDtypeStruct((places, shared), BF16),
            jax.ShapeDtypeStruct((places, direct), BF16),
        ],
        (shortcut, moe_gain, ids),
        2 * places * rows * (shared + direct),
    )
    arrived = to_owners(outgoing)
    received = swapped(arrived)
    arrived_both = to_owners(outgoing_both)
    (combine,) = call(
        combine_map_body,
        [jax.ShapeDtypeStruct((rows, places), BF16)],
        (shortcut, moe_gain, router_weight, ids),
        2 * rows * 128 * d_model,
        cost=0,
    )
    (acc,) = call(
        first_part_body,
        [jax.ShapeDtypeStruct((places, ff2), F32)],
        (arrived, gate_up_weight),
        2 * places * shared * ff2,
        specs=[vmem(), anywhere()],
        scratch=[pltpu.VMEM((shared, ff2), BF16), pltpu.SemaphoreType.DMA],
    )
    out_both, handed, kept = call(
        expert_body,
        [
            jax.ShapeDtypeStruct((places, direct), BF16),
            jax.ShapeDtypeStruct((places, shared), BF16),
            jax.ShapeDtypeStruct((places, shared), BF16),
        ],
        (acc, received, arrived_both, gate_up_weight, down_weight, near),
        2 * places * (shared + direct) * ff2 + 2 * places * ff * d_model,
        specs=[anywhere()] * 6,
        out_specs=[anywhere()] * 3,
        scratch=[
            pltpu.VMEM((places, ff2), F32),
            pltpu.VMEM((places, shared + direct), BF16),
            pltpu.VMEM((shared + direct, ff2), BF16),
            pltpu.VMEM((ff, d_model), BF16),
            pltpu.VMEM((places, ff), BF16),
            pltpu.VMEM((places, direct), BF16),
            pltpu.VMEM((places, shared), BF16),
            pltpu.VMEM((places, shared), BF16),
            pltpu.SemaphoreType.DMA((11,)),
        ],
    )
    across = lax.ppermute(near, "ep", [(i, i ^ 16) for i in range(n_ep)])
    cores = [(i, i ^ 1) for i in range(n_ep)]
    other_near = lax.ppermute(near, "ep", cores)
    got = swapped(handed)
    returned_both = to_owners(out_both)
    expert_out = (kept.astype(F32) + got.astype(F32)).astype(BF16)
    returned = to_owners(expert_out)
    (across,) = call(
        relay_body,
        [jax.ShapeDtypeStruct(across.shape, BF16)],
        (across, expert_out),
        0,
        cost=0,
        specs=[anywhere()] * 2,
        out_specs=[anywhere()],
        aliases={0: 0},
    )
    other_across = lax.ppermute(across, "ep", cores)

    position = jnp.arange(rows, dtype=F32)
    freq = ROPE_BASE ** (-jnp.arange(HD // 2, dtype=F32) * 2.0 / HD)
    angle = position[:, None] * freq[None, :]
    cosine, sine = jnp.cos(angle), jnp.sin(angle)
    cosine = jnp.concatenate([cosine, cosine], 1)
    sine = jnp.concatenate([-sine, sine], 1)
    att_handed, att_kept, att_both = call(
        attention_body,
        [
            jax.ShapeDtypeStruct((rows, shared), BF16),
            jax.ShapeDtypeStruct((rows, shared), F32),
            jax.ShapeDtypeStruct((rows, direct), F32),
        ],
        (
            residual_in,
            attn_gain[None, :],
            near,
            across,
            other_near,
            other_across,
            query_gain[None, :],
            key_gain[None, :],
            cosine,
            sine,
        ),
        2 * rows * d_model * packed.shape[1],
        cost=0,
        scratch=[pltpu.VMEM((d_model, packed.shape[1]), BF16)],
    )
    att_got = swapped(att_handed)
    (total,) = call(
        combine_body,
        [jax.ShapeDtypeStruct((rows, shared + direct), BF16)],
        (combine, returned, returned_both, att_kept, att_got, att_both),
        2 * rows * places * (shared + direct),
        specs=[vmem()] * 6,
    )
    share = rows // n_tp
    terms = lax.all_to_all(
        total.reshape(n_tp, share, shared + direct),
        "tp",
        split_axis=0,
        concat_axis=0,
        tiled=True,
    )
    terms = terms.astype(F32)
    sums = [jnp.sum(terms[h::2, :, :shared], 0) for h in range(2)]
    sums = jnp.concatenate(sums + [jnp.sum(terms[:, :, shared:], 0)], 1)
    own = lax.dynamic_slice_in_dim(residual_in, rank * share, share, 0)
    mine = (own.astype(F32) + sums).astype(BF16)
    everyone = lax.all_to_all(
        jnp.broadcast_to(mine[None], (n_tp, share, d_model)),
        "tp",
        split_axis=0,
        concat_axis=0,
        tiled=True,
    )
    return everyone.reshape(rows, d_model)


def solution(mesh):
    return jax.shard_map(
        local,
        mesh=mesh,
        in_specs=(
            P("ep", None),
            P("ep", None),
            P(),
            P(),
            P("ep", "tp"),
            P("ep", None),
            P("ep", "tp"),
            P(),
            P(),
            P(),
            P("ep", None),
            P(("ep", "tp"), None, None),
            P(("ep", "tp"), None, None),
        ),
        out_specs=P("ep", None),
        check_vma=False,
    )
```

time: 196 us -> 183 us (0.934)
  blocking collectives: 63.4 us -> 17 us
  starting transfers between devices: 19.4 us -> 37.9 us
  waiting for transfers between devices: 62.3 us -> 73 us
  Pallas kernels: 21.8 us -> 30.9 us
  local copies, waits for them, and re-layouts: 10.6 us -> 4.57 us
    all_to_all x2 -> x1, blocking collectives: 63.4 us -> 17 us  [local(): lax.all_to_all(jnp.broadcast_to(mine[None], (n_tp, share, d_model)), 'tp'...]
    ppermute x3 -> x6, waiting for transfers between devices: 37.4 us -> 12.8 us  [the longest x3 10.8 us: swapped(): return lax.ppermute(value, 'tp', partner)]
    all_to_all x2 -> x5, waiting for transfers between devices: 24.8 us -> 44.8 us  [the longest x4 34.2 us: to_owners(): return lax.all_to_all(value, 'ep', split_axis=0, concat_axis=0, tiled=True)]
    all_to_all x2 -> x5, starting transfers between devices: 14.6 us -> 31.3 us  [the longest x4 25 us: to_owners(): return lax.all_to_all(value, 'ep', split_axis=0, concat_axis=0, tiled=True)]
    all_gather x1, waiting for transfers between devices: 0.01 us -> 15.4 us  [local(): lax.all_gather(packed, 'ep', axis=0, tiled=True, axis_index_groups=along_z)]
    pallas_call x6 -> x7, Pallas kernels: 21.8 us -> 30.9 us  [call(): pl.pallas_call(body, out_shape=out_shape, in_specs=specs or [vmem()] * le...]
    unnamed x30 -> x19, local copies, waits for them, and re-layouts: 8.94 us -> 3.75 us
    convert_element_type x2 -> x3, other arithmetic: 1.36 us -> 3.42 us  [the longest x1 2.43 us: local(): expert_out = (kept.astype(F32) + got.astype(F32)).astype(BF16)]
  transfers between devices with their start and end apart: 6 -> 12, of which waited for: 4 -> 7; matrix products, arithmetic and copies ran while one was open for 2% -> 3% of each run, Pallas kernels for 10% -> 14%
where the time goes in v2:
time: 183 us; the launch traced here: 182 us
  waiting for transfers between devices  73 us (40%)
  starting transfers between devices  37.9 us (21%)
  Pallas kernels  30.9 us (17%)
  blocking collectives  17 us (9%)
  between operations  13.5 us (7%)
  other arithmetic  5.36 us (3%)
  local copies, waits for them, and re-layouts  4.57 us (2%)
    all_to_all x4, waiting for transfers between devices, to_owners(): return lax.all_to_all(value, 'ep', split_axis=0, concat_axis=0, tiled=True)  34.2 us
    pallas_call x7, Pallas kernels, call(): pl.pallas_call(body, out_shape=out_shape, in_specs=specs or [vmem()] * le...  30.9 us
    all_to_all x4, starting transfers between devices, to_owners(): return lax.all_to_all(value, 'ep', split_axis=0, concat_axis=0, tiled=True)  25 us
    all_to_all x1, blocking collectives, local(): lax.all_to_all(jnp.broadcast_to(mine[None], (n_tp, share, d_model)), 'tp'...  17 us
    all_gather x1, waiting for transfers between devices, local(): lax.all_gather(packed, 'ep', axis=0, tiled=True, axis_index_groups=along_z)  15.4 us
    ppermute x3, waiting for transfers between devices, swapped(): return lax.ppermute(value, 'tp', partner)  10.8 us
    all_to_all x1, waiting for transfers between devices, local(): lax.all_to_all(total.reshape(n_tp, share, shared + direct), 'tp', split_a...  10.5 us
    all_to_all x1, starting transfers between devices, local(): lax.all_to_all(total.reshape(n_tp, share, shared + direct), 'tp', split_a...  6.3 us
  transfers between devices with their start and end apart: 12, of which 7 were waited for; matrix products, arithmetic and copies ran while one was open for 3% of the time, Pallas kernels for 14%

profile of v2, /device:TPU:32, one launch (start us, length us, event | category | flops | bytes accessed | tf_op | source)
XLA Modules:
  0.0 182.2 jit_solution(9602707266228118467)
XLA Ops:
  6.5 3.1 %shard_map.128 = (bf16[512,768]{1,0:T(8,128)(2,1)}, bf16[512,512]{1,0:T(8,128)(2,1)}) custom-call(bf16[192,2048]{1,0:T(8,128)(2,1)} %rows_ref.4, f32[1,2048]{1,0:T(1,128)} %bitcast.25, s32[8,192]{1,0:T(8,128)} %bitcast.27), custom_call_target="tpu_custom_call" | custom-call | flops 251658240 | bytes 2111488 | tf_op jit(solution)/shard_map/pallas_call | solution.py:35
  9.6 9.7 %all-to-all-start = ((bf16[32,16,768]{2,1,0:T(8,128)(2,1)}), bf16[32,16,768]{2,1,0:T(8,128)(2,1)S(1)}, u32[]{:S(2)}, u32[]{:S(2)}) async-start(bf16[32,16,768]{2,1,0:T(8,128)(2,1)} %bitcast.22), calls=%async_computation | async-start | bytes 1572864 | tf_op jit(solution)/shard_map/all_to_all | solution.py:297
  19.3 0.0 all-gather.2.cloned.1.call-start
  19.3 0.7 constant_dynamic-slice_fusion.1
  20.1 0.0 copy-done.8
  20.1 0.0 copy-done.7
  20.1 0.7 pad_maximum_fusion
  20.8 0.0 all-gather.2.cloned.1.call-update
  20.8 23.0 %all-to-all-done = bf16[32,16,768]{2,1,0:T(8,128)(2,1)S(1)} async-done(((bf16[32,16,768]{2,1,0:T(8,128)(2,1)}), bf16[32,16,768]{2,1,0:T(8,128)(2,1)S(1)}, u32[]{:S(2)}, u32[]{:S(2)}) %all-to-all-start) | async-done | bytes 786464 | tf_op jit(solution)/shard_map/all_to_all | solution.py:297
  43.7 3.9 %all-to-all-start.1 = ((bf16[32,16,512]{2,1,0:T(8,128)(2,1)}), bf16[32,16,512]{2,1,0:T(8,128)(2,1)S(1)}, u32[]{:S(2)}, u32[]{:S(2)}) async-start(bf16[32,16,512]{2,1,0:T(8,128)(2,1)} %bitcast.4), calls=%async_computation.1 | async-start | bytes 1048576 | tf_op jit(solution)/shard_map/all_to_all | solution.py:297
  47.7 1.7 collective-permute-start
  49.4 5.8 %shard_map.129.acc_ref = f32[512,1536]{1,0:T(8,128)} custom-call(bf16[512,768]{1,0:T(8,128)(2,1)} %bitcast.16, bf16[1,2048,1536]{2,1,0:T(8,128)(2,1)} %w_ref.3), custom_call_target="tpu_custom_call" | custom-call | flops 1207959552 | bytes 10223616 | tf_op jit(solution)/shard_map/pallas_call | solution.py:35
  55.2 15.4 %all-gather.2.cloned.1.call-done.near_ref = bf16[512,1280]{1,0:T(8,128)(2,1)} async-done(((bf16[64,1280]{1,0:T(8,128)(2,1)}), bf16[512,1280]{1,0:T(8,128)(2,1)}) %all-gather.2.cloned.1.call-update) | async-done | bytes 1310736 | tf_op jit(solution)/shard_map/all_gather | solution.py:294
  70.6 1.3 collective-permute-start.2
  72.0 0.0 all-to-all-done.1
  72.0 0.0 collective-permute-done.got_ref
  72.0 0.8 copy-done.5
  72.8 8.6 %shard_map.130 = (bf16[512,512]{1,0:T(8,128)(2,1)}, bf16[512,768]{1,0:T(8,128)(2,1)}, bf16[512,768]{1,0:T(8,128)(2,1)}) custom-call(f32[512,1536]{1,0:T(8,128)} %shard_map.129.acc_ref, bf16[512,768]{1,0:T(8,128)(2,1)} %collective-permute-done.got_ref, bf16[512,512]{1,0:T(8,128)(2,1)} %bitcast.20, bf16[1,2048,1536]{2,1,0:T(8,128)(2,1)} %w_ref.3, ...), custom_call_target="tpu_custom_call" | custom-call | flops 3623878656 | bytes 17301504 | tf_op jit(solution)/shard_map/pallas_call | solution.py:35
  81.3 1.7 collective-permute-start.1
  83.0 4.8 %all-to-all-start.3 = ((bf16[32,16,512]{2,1,0:T(8,128)(2,1)}), bf16[32,16,512]{2,1,0:T(8,128)(2,1)S(1)}, u32[]{:S(2)}, u32[]{:S(2)}) async-start(bf16[32,16,512]{2,1,0:T(8,128)(2,1)} %bitcast.23), calls=%async_computation.3 | async-start | bytes 1048576 | tf_op jit(solution)/shard_map/all_to_all | solution.py:297
  87.8 0.2 collective-permute-start.3
  88.1 10.8 %collective-permute-done.1 = bf16[512,768]{1,0:T(8,128)(2,1)} collective-permute-done((bf16[512,768]{1,0:T(8,128)(2,1)}, bf16[512,768]{1,0:T(8,128)(2,1)}, u32[]{:S(2)}, u32[]{:S(2)}) %collective-permute-start.1) | collective-permute-done | bytes 786464 | tf_op jit(solution)/shard_map/ppermute | solution.py:300
  98.9 2.4 %add_convert_fusion.after_ref = bf16[512,768]{1,0:T(8,128)(2,1)} fusion(bf16[512,768]{1,0:T(8,128)(2,1)} %collective-permute-done.1, bf16[512,768]{1,0:T(8,128)(2,1)} %get-tuple-element.15), kind=kLoop, calls=%fused_computation | loop fusion | flops 1572864 | bytes 2359296 | tf_op jit(solution)/shard_map/convert_element_type | solution.py:359
  101.3 1.9 %collective-permute-done.2.value_ref = bf16[512,1280]{1,0:T(8,128)(2,1)S(1)} collective-permute-done((bf16[512,1280]{1,0:T(8,128)(2,1)}, bf16[512,1280]{1,0:T(8,128)(2,1)S(1)}, u32[]{:S(2)}, u32[]{:S(2)}) %collective-permute-start.2) | collective-permute-done | bytes 1310752 | tf_op jit(solution)/shard_map/ppermute | solution.py:354
  103.3 1.1 copy-done
  104.4 0.0 collective-permute-start.4
  104.4 1.2 all-to-all-done.3
  105.6 6.6 %all-to-all-start.2 = ((bf16[32,16,768]{2,1,0:T(8,128)(2,1)}), bf16[32,16,768]{2,1,0:T(8,128)(2,1)S(1)}, u32[]{:S(2)}, u32[]{:S(2)}) async-start(bf16[32,16,768]{2,1,0:T(8,128)(2,1)} %bitcast.6), calls=%async_computation.2 | async-start | bytes 1572864 | tf_op jit(solution)/shard_map/all_to_all | solution.py:297
  112.2 0.4 fusion.3
  112.6 0.8 pad_maximum_fusion.1
  113.4 0.0 collective-permute-done.3.other_near_ref
  113.4 0.0 collective-permute-done.4.other_across_ref
  113.4 7.4 %shard_map.132 = (bf16[192,768]{1,0:T(8,128)(2,1)}, f32[192,768]{1,0:T(8,128)}, f32[192,512]{1,0:T(8,128)}) custom-call(bf16[192,2048]{1,0:T(8,128)(2,1)} %rows_ref.5, f32[1,2048]{1,0:T(1,128)} %bitcast.24, bf16[512,1280]{1,0:T(8,128)(2,1)} %all-gather.2.cloned.1.call-done.near_ref, bf16[512,1280]{1,0:T(8,128)(2,1)} %shard_map.131.across_ref, ...), custom_call_target="tpu_custom_call" | custom-call | tf_op jit(solution)/shard_map/pallas_call | solution.py:35
  120.8 0.0 copy-done.4
  120.8 1.6 collective-permute-start.5
  122.4 3.1 %shard_map.127.map_ref = bf16[192,512]{1,0:T(8,128)(2,1)} custom-call(bf16[192,2048]{1,0:T(8,128)(2,1)} %rows_ref.4, f32[1,2048]{1,0:T(1,128)} %bitcast.26, bf16[128,2048]{1,0:T(8,128)(2,1)} %router_ref.1, s32[8,192]{1,0:T(8,128)} %bitcast.28), custom_call_target="tpu_custom_call" | custom-call | tf_op jit(solution)/shard_map/pallas_call | solution.py:35
  125.5 10.1 %all-to-all-done.2 = bf16[32,16,768]{2,1,0:T(8,128)(2,1)S(1)} async-done(((bf16[32,16,768]{2,1,0:T(8,128)(2,1)}), bf16[32,16,768]{2,1,0:T(8,128)(2,1)S(1)}, u32[]{:S(2)}, u32[]{:S(2)}) %all-to-all-start.2) | async-done | bytes 786464 | tf_op jit(solution)/shard_map/all_to_all | solution.py:297
  135.6 0.0 collective-permute-done.5.got_ref
  135.6 0.9 copy-done.3
  136.4 0.1 copy-done.6
  136.5 3.0 %shard_map.133 = bf16[192,1280]{1,0:T(8,128)(2,1)} custom-call(bf16[192,512]{1,0:T(8,128)(2,1)} %shard_map.127.map_ref, bf16[512,768]{1,0:T(8,128)(2,1)} %bitcast.18, bf16[512,512]{1,0:T(8,128)(2,1)} %bitcast.19, f32[192,768]{1,0:T(8,128)} %get-tuple-element.18.kept_ref, bf16[192,768]{1,0:T(8,128)(2,1)} %copy-done.6, f32[192,512]{1,0:T(8,128)} %get-tuple-element.20.direct_ref), custom_call_target="tpu_custom_call" | custom-call | flops 251658240 | bytes 3276800 | tf_op jit(solution)/shard_map/pallas_call | solution.py:35
  139.5 6.3 %all-to-all-start.4 = ((bf16[8,24,1280]{2,1,0:T(8,128)(2,1)}), bf16[8,24,1280]{2,1,0:T(8,128)(2,1)S(1)}, u32[]{:S(2)}, u32[]{:S(2)}) async-start(bf16[8,24,1280]{2,1,0:T(8,128)(2,1)} %bitcast.21), calls=%async_computation.4 | async-start | bytes 983040 | tf_op jit(solution)/shard_map/all_to_all | solution.py:411
  145.8 10.5 %all-to-all-done.4 = bf16[8,24,1280]{2,1,0:T(8,128)(2,1)S(1)} async-done(((bf16[8,24,1280]{2,1,0:T(8,128)(2,1)}), bf16[8,24,1280]{2,1,0:T(8,128)(2,1)S(1)}, u32[]{:S(2)}, u32[]{:S(2)}) %all-to-all-start.4) | async-done | bytes 491552 | tf_op jit(solution)/shard_map/all_to_all | solution.py:411
  156.3 0.1 convert_element_type.22
  156.5 0.9 fusion
  157.4 0.1 broadcast_in_dim.24
  157.5 17.0 %all_to_all.54 = bf16[8,24,2048]{2,1,0:T(8,128)(2,1)S(1)} all-to-all(bf16[8,24,2048]{2,1,0:T(8,128)(2,1)S(1)} %broadcast_in_dim.24), channel_id=1, replica_groups=mesh['ep'=32,'tp'=8] {'tp'}, dimensions={0} | all-to-all | bytes 1572864 | tf_op jit(solution)/shard_map/all_to_all | solution.py:423
  174.5 0.9 copy.17
  (15 shorter events, 0.1 us)
Async XLA Ops:
  6.5 13.6 %copy-start.8 = (bf16[64,512]{1,0:T(8,128)(2,1)S(1)}, bf16[64,512]{1,0:T(8,128)(2,1)}, u32[]{:S(2)}) copy-start(bf16[64,512]{1,0:T(8,128)(2,1)} %param.17) | copy-start | bytes 196612
  6.5 13.6 %copy-start.7 = (bf16[64,512]{1,0:T(8,128)(2,1)S(1)}, bf16[64,512]{1,0:T(8,128)(2,1)}, u32[]{:S(2)}) copy-start(bf16[64,512]{1,0:T(8,128)(2,1)} %param.19) | copy-start | bytes 196612
  9.6 34.1 %all-to-all-start = ((bf16[32,16,768]{2,1,0:T(8,128)(2,1)}), bf16[32,16,768]{2,1,0:T(8,128)(2,1)S(1)}, u32[]{:S(2)}, u32[]{:S(2)}) async-start(bf16[32,16,768]{2,1,0:T(8,128)(2,1)} %bitcast.22), calls=%async_computation | async-start | bytes 1572864 | tf_op jit(solution)/shard_map/all_to_all | solution.py:297
  19.3 51.4 %all-gather.2.cloned.1.call-start = ((), (), s32[]{:S(2)}) async-start(), calls=%async_computation.6 | async-start | bytes 1474560 | tf_op jit(solution)/shard_map/all_gather | solution.py:294
  43.7 5.7 %copy-start.2 = (bf16[32,16,768]{2,1,0:T(8,128)(2,1)}, bf16[32,16,768]{2,1,0:T(8,128)(2,1)S(1)}, u32[]{:S(2)}) copy-start(bf16[32,16,768]{2,1,0:T(8,128)(2,1)S(1)} %all-to-all-done) | copy-start | bytes 2359300
  43.7 28.2 %all-to-all-start.1 = ((bf16[32,16,512]{2,1,0:T(8,128)(2,1)}), bf16[32,16,512]{2,1,0:T(8,128)(2,1)S(1)}, u32[]{:S(2)}, u32[]{:S(2)}) async-start(bf16[32,16,512]{2,1,0:T(8,128)(2,1)} %bitcast.4), calls=%async_computation.1 | async-start | bytes 1048576 | tf_op jit(solution)/shard_map/all_to_all | solution.py:297
  47.7 24.3 %collective-permute-start = (bf16[512,768]{1,0:T(8,128)(2,1)S(1)}, bf16[512,768]{1,0:T(8,128)(2,1)}, u32[]{:S(2)}, u32[]{:S(2)}) collective-permute-start(bf16[512,768]{1,0:T(8,128)(2,1)S(1)} %bitcast.15), channel_id=1, source_target_pairs={{0,1},{1,0},{2,3},{3,2},{4,5},{5,4},{6,7},{7,6},{8,9},{9,8},{10,11... | collective-permute-start | bytes 2359304 | tf_op jit(solution)/shard_map/ppermute | solution.py:300
  70.6 32.6 %collective-permute-start.2 = (bf16[512,1280]{1,0:T(8,128)(2,1)}, bf16[512,1280]{1,0:T(8,128)(2,1)S(1)}, u32[]{:S(2)}, u32[]{:S(2)}) collective-permute-start(bf16[512,1280]{1,0:T(8,128)(2,1)} %all-gather.2.cloned.1.call-done.near_ref), channel_id=1, source_target_pairs={{0,128},{8,136},{16,144},{24,152},{32,160},{40,168},{48,176},{56,1... | collective-permute-start | bytes 3932168 | tf_op jit(solution)/shard_map/ppermute | solution.py:354
  72.0 0.8 copy-start.5
  72.8 15.0 %copy-start.1 = (bf16[512,1280]{1,0:T(8,128)(2,1)S(1)}, bf16[512,1280]{1,0:T(8,128)(2,1)}, u32[]{:S(2)}) copy-start(bf16[512,1280]{1,0:T(8,128)(2,1)} %all-gather.2.cloned.1.call-done.near_ref) | copy-start | bytes 3932164
  81.3 17.6 %collective-permute-start.1 = (bf16[512,768]{1,0:T(8,128)(2,1)}, bf16[512,768]{1,0:T(8,128)(2,1)}, u32[]{:S(2)}, u32[]{:S(2)}) collective-permute-start(bf16[512,768]{1,0:T(8,128)(2,1)} %get-tuple-element.16), channel_id=1, source_target_pairs={{0,1},{1,0},{2,3},{3,2},{4,5},{5,4},{6,7},{7,6},{8,9},{9,8},{10,11... | collective-permute-start | bytes 2359304 | tf_op jit(solution)/shard_map/ppermute | solution.py:300
  83.0 22.5 %all-to-all-start.3 = ((bf16[32,16,512]{2,1,0:T(8,128)(2,1)}), bf16[32,16,512]{2,1,0:T(8,128)(2,1)S(1)}, u32[]{:S(2)}, u32[]{:S(2)}) async-start(bf16[32,16,512]{2,1,0:T(8,128)(2,1)} %bitcast.23), calls=%async_computation.3 | async-start | bytes 1048576 | tf_op jit(solution)/shard_map/all_to_all | solution.py:297
  87.8 25.6 %collective-permute-start.3 = (bf16[512,1280]{1,0:T(8,128)(2,1)S(1)}, bf16[512,1280]{1,0:T(8,128)(2,1)}, u32[]{:S(2)}, u32[]{:S(2)}) collective-permute-start(bf16[512,1280]{1,0:T(8,128)(2,1)S(1)} %copy-done.1), channel_id=1, source_target_pairs={{0,8},{8,0},{16,24},{24,16},{32,40},{40,32},{48,56},{56,48},{64,72... | collective-permute-start | bytes 3932168 | tf_op jit(solution)/shard_map/ppermute | solution.py:356
  103.3 1.1 copy-start
  104.4 9.1 %collective-permute-start.4 = (bf16[512,1280]{1,0:T(8,128)(2,1)}, bf16[512,1280]{1,0:T(8,128)(2,1)}, u32[]{:S(2)}, u32[]{:S(2)}) collective-permute-start(bf16[512,1280]{1,0:T(8,128)(2,1)} %shard_map.131.across_ref), channel_id=1, source_target_pairs={{0,8},{8,0},{16,24},{24,16},{32,40},{40,32},{48,56},{56,48},{64,72... | collective-permute-start | bytes 3932168 | tf_op jit(solution)/shard_map/ppermute | solution.py:371
  105.6 15.2 %copy-start.4 = (bf16[32,16,512]{2,1,0:T(8,128)(2,1)}, bf16[32,16,512]{2,1,0:T(8,128)(2,1)S(1)}, u32[]{:S(2)}) copy-start(bf16[32,16,512]{2,1,0:T(8,128)(2,1)S(1)} %all-to-all-done.3) | copy-start | bytes 1572868
  105.6 30.0 %all-to-all-start.2 = ((bf16[32,16,768]{2,1,0:T(8,128)(2,1)}), bf16[32,16,768]{2,1,0:T(8,128)(2,1)S(1)}, u32[]{:S(2)}, u32[]{:S(2)}) async-start(bf16[32,16,768]{2,1,0:T(8,128)(2,1)} %bitcast.6), calls=%async_computation.2 | async-start | bytes 1572864 | tf_op jit(solution)/shard_map/all_to_all | solution.py:297
  120.8 14.8 %collective-permute-start.5 = (bf16[192,768]{1,0:T(8,128)(2,1)}, bf16[192,768]{1,0:T(8,128)(2,1)S(1)}, u32[]{:S(2)}, u32[]{:S(2)}) collective-permute-start(bf16[192,768]{1,0:T(8,128)(2,1)} %get-tuple-element.19), channel_id=1, source_target_pairs={{0,1},{1,0},{2,3},{3,2},{4,5},{5,4},{6,7},{7,6},{8,9},{9,8},{10,11... | collective-permute-start | bytes 884744 | tf_op jit(solution)/shard_map/ppermute | solution.py:300
  135.6 0.9 copy-start.3
  135.6 1.0 copy-start.6
  139.5 16.8 %all-to-all-start.4 = ((bf16[8,24,1280]{2,1,0:T(8,128)(2,1)}), bf16[8,24,1280]{2,1,0:T(8,128)(2,1)S(1)}, u32[]{:S(2)}, u32[]{:S(2)}) async-start(bf16[8,24,1280]{2,1,0:T(8,128)(2,1)} %bitcast.21), calls=%async_computation.4 | async-start | bytes 983040 | tf_op jit(solution)/shard_map/all_to_all | solution.py:411
Sparse Core Ops, SparseCore 0:
  21.9 48.6 all-gather.1

commit v3 on v2

--- a/solution.py
+++ b/solution.py
@@ -18,7 +18,6 @@
 F32 = jnp.float32
 BF16 = jnp.bfloat16
 NT = (((1,), (1,)), ((), ()))
-VMEM_LIMIT = 56 * 1024 * 1024
 
 
 def vmem():
@@ -29,7 +28,7 @@
     return pl.BlockSpec(memory_space=pl.ANY)
 
 
-def call(body, out_shape, args, flops, extra_bytes=0, scratch=(), specs=None, out_specs=None, aliases=None, cost=None):
+def call(body, out_shape, args, flops, extra_bytes=0, scratch=(), specs=None, out_specs=None, aliases=None, cost=None, limit=56):
     moved = extra_bytes + sum(a.size * a.dtype.itemsize for a in args)
     moved += sum(o.size * o.dtype.itemsize for o in out_shape)
     return pl.pallas_call(
@@ -39,7 +38,7 @@
         out_specs=out_specs or [vmem()] * len(out_shape),
         scratch_shapes=list(scratch),
         input_output_aliases=aliases or {},
-        compiler_params=pltpu.CompilerParams(vmem_limit_bytes=VMEM_LIMIT),
+        compiler_params=pltpu.CompilerParams(vmem_limit_bytes=limit * 1024 * 1024),
         cost_estimate=pl.CostEstimate(
             flops=flops if cost is None else cost,
             bytes_accessed=moved if cost is None else cost,
@@ -134,28 +133,37 @@
     sems,
 ):
     side = lax.axis_index("tp") % 2
-    width = out_kept.shape[1]
-    mine = pl.multiple_of(side * width, width)
+    used = iter(range(32))
+
+    def started(source, target):
+        copy = pltpu.make_async_copy(source, target, sems.at[next(used)])
+        copy.start()
+        return copy
+
+    width = got_ref.shape[1]
     other = pl.multiple_of((1 - side) * width, width)
     ff = hidden.shape[1]
     tile = 256
-    moves = [
-        (got_ref, x_buf.at[:, :width]),
-        (both_ref, x_buf.at[:, width:]),
-    ]
-    for start in (0, ff):
-        columns = pl.ds(start, ff)
-        moves.append((w_ref.at[0, pl.ds(other, width), columns], w_buf.at[:width, columns]))
-        moves.append((w_ref.at[0, 2 * width :, columns], w_buf.at[width:, columns]))
-    moves.append((acc_ref, acc))
-    moves.append((down_ref.at[0], w_down))
-    copies = [pltpu.make_async_copy(a, b, sems.at[i]) for i, (a, b) in enumerate(moves)]
-    for copy in copies:
-        copy.start()
-    for copy in copies[:-1]:
+    inputs = [started(got_ref, x_buf.at[:, :width]), started(both_ref, x_buf.at[:, width:])]
+    strips = []
+    for at in range(0, ff, tile):
+        strip = []
+        for start in (at, ff + at):
+            columns = pl.ds(start, tile)
+            strip += [
+                started(w_ref.at[0, pl.ds(other, width), columns], w_buf.at[:width, columns]),
+                started(w_ref.at[0, 2 * width :, columns], w_buf.at[width:, columns]),
+                started(acc_ref.at[:, columns], acc.at[:, columns]),
+            ]
+        strips.append(strip)
+    last = started(down_ref.at[0], w_down)
+    for copy in inputs:
         copy.wait()
     x = x_buf[...]
-    for at in range(0, ff, tile):
+    for step, strip in enumerate(strips):
+        for copy in strip:
+            copy.wait()
+        at = step * tile
         gate = acc[:, at : at + tile] + jnp.dot(
             x, w_buf[:, at : at + tile], preferred_element_type=F32
         )
@@ -163,20 +171,20 @@
             x, w_buf[:, ff + at : ff + at + tile], preferred_element_type=F32
         )
         hidden[:, at : at + tile] = (jax.nn.silu(gate) * up).astype(BF16)
-    copies[-1].wait()
+    last.wait()
+    width = out_kept.shape[1]
+    mine = pl.multiple_of(side * width, width)
+    other = pl.multiple_of((1 - side) * width, width)
 
     def projected(columns):
         return jnp.dot(hidden[...], w_down[:, columns], preferred_element_type=F32).astype(BF16)
 
     out_handed[...] = projected(pl.ds(other, width))
-    back = [pltpu.make_async_copy(out_handed, handed_ref, sems.at[8])]
-    back[0].start()
+    back = [started(out_handed, handed_ref)]
     out_direct[...] = projected(pl.ds(2 * width, out_direct.shape[1]))
-    back.append(pltpu.make_async_copy(out_direct, direct_ref, sems.at[9]))
-    back[1].start()
+    back.append(started(out_direct, direct_ref))
     out_kept[...] = projected(pl.ds(mine, width))
-    back.append(pltpu.make_async_copy(out_kept, kept_ref, sems.at[10]))
-    back[2].start()
+    back.append(started(out_kept, kept_ref))
     for copy in back:
         copy.wait()
 
@@ -278,6 +286,8 @@
     n_tp = lax.axis_size("tp")
     rank = lax.axis_index("tp")
     rows, d_model = residual_in.shape
+    direct_in = d_model // 8
+    shared_in = (d_model - direct_in) // 2
     direct = d_model // 4
     shared = (d_model - direct) // 2
     places = n_ep * SLOTS
@@ -304,11 +314,11 @@
     outgoing, outgoing_both = call(
         dispatch_body,
         [
-            jax.ShapeDtypeStruct((places, shared), BF16),
-            jax.ShapeDtypeStruct((places, direct), BF16),
+            jax.ShapeDtypeStruct((places, shared_in), BF16),
+            jax.ShapeDtypeStruct((places, direct_in), BF16),
         ],
         (shortcut, moe_gain, ids),
-        2 * places * rows * (shared + direct),
+        2 * places * rows * (shared_in + direct_in),
     )
     arrived = to_owners(outgoing)
     received = swapped(arrived)
@@ -324,9 +334,9 @@
         first_part_body,
         [jax.ShapeDtypeStruct((places, ff2), F32)],
         (arrived, gate_up_weight),
-        2 * places * shared * ff2,
+        2 * places * shared_in * ff2,
         specs=[vmem(), anywhere()],
-        scratch=[pltpu.VMEM((shared, ff2), BF16), pltpu.SemaphoreType.DMA],
+        scratch=[pltpu.VMEM((shared_in, ff2), BF16), pltpu.SemaphoreType.DMA],
     )
     out_both, handed, kept = call(
         expert_body,
@@ -336,19 +346,19 @@
             jax.ShapeDtypeStruct((places, shared), BF16),
         ],
         (acc, received, arrived_both, gate_up_weight, down_weight, near),
-        2 * places * (shared + direct) * ff2 + 2 * places * ff * d_model,
+        2 * places * (shared_in + direct_in) * ff2 + 2 * places * ff * d_model,
         specs=[anywhere()] * 6,
         out_specs=[anywhere()] * 3,
         scratch=[
             pltpu.VMEM((places, ff2), F32),
-            pltpu.VMEM((places, shared + direct), BF16),
-            pltpu.VMEM((shared + direct, ff2), BF16),
+            pltpu.VMEM((places, shared_in + direct_in), BF16),
+            pltpu.VMEM((shared_in + direct_in, ff2), BF16),
             pltpu.VMEM((ff, d_model), BF16),
             pltpu.VMEM((places, ff), BF16),
             pltpu.VMEM((places, direct), BF16),
             pltpu.VMEM((places, shared), BF16),
             pltpu.VMEM((places, shared), BF16),
-            pltpu.SemaphoreType.DMA((11,)),
+            pltpu.SemaphoreType.DMA((32,)),
         ],
     )
     across = lax.ppermute(near, "ep", [(i, i ^ 16) for i in range(n_ep)])
@@ -364,6 +374,7 @@
         (across, expert_out),
         0,
         cost=0,
+        limit=1,
         specs=[anywhere()] * 2,
         out_specs=[anywhere()],
         aliases={0: 0},
@@ -405,7 +416,7 @@
         [jax.ShapeDtypeStruct((rows, shared + direct), BF16)],
         (combine, returned, returned_both, att_kept, att_got, att_both),
         2 * rows * places * (shared + direct),
-        specs=[vmem()] * 6,
+        limit=16,
     )
     share = rows // n_tp
     terms = lax.all_to_all(

time: 183 us -> 179 us (0.978)
  Pallas kernels: 30.9 us -> 28.6 us
    all_gather x1, waiting for transfers between devices: 15.4 us -> 8.26 us  [local(): lax.all_gather(packed, 'ep', axis=0, tiled=True, axis_index_groups=along_z)]
    all_to_all x4, waiting for transfers between devices: 34.2 us -> 40.5 us  [to_owners(): return lax.all_to_all(value, 'ep', split_axis=0, concat_axis=0, tiled=True)]
    pallas_call x7, Pallas kernels: 30.9 us -> 28.6 us  [call(): pl.pallas_call(body, out_shape=out_shape, in_specs=specs or [vmem()] * le...]
    unnamed x19 -> x21, local copies, waits for them, and re-layouts: 3.75 us -> 2.87 us
where the time goes in v3:
time: 179 us; the launch traced here: 178 us
  waiting for transfers between devices  72.2 us (40%)
  starting transfers between devices  37.6 us (21%)
  Pallas kernels  28.6 us (16%)
  blocking collectives  17 us (9%)
  between operations  13.6 us (8%)
  other arithmetic  5.12 us (3%)
  local copies, waits for them, and re-layouts  3.69 us (2%)
    all_to_all x4, waiting for transfers between devices, to_owners(): return lax.all_to_all(value, 'ep', split_axis=0, concat_axis=0, tiled=True)  40.5 us
    pallas_call x7, Pallas kernels, call(): pl.pallas_call(body, out_shape=out_shape, in_specs=specs or [vmem()] * le...  28.6 us
    all_to_all x4, starting transfers between devices, to_owners(): return lax.all_to_all(value, 'ep', split_axis=0, concat_axis=0, tiled=True)  25.4 us
    all_to_all x1, blocking collectives, local(): lax.all_to_all(jnp.broadcast_to(mine[None], (n_tp, share, d_model)), 'tp'...  17 us
    ppermute x3, waiting for transfers between devices, swapped(): return lax.ppermute(value, 'tp', partner)  11.1 us
    all_to_all x1, waiting for transfers between devices, local(): lax.all_to_all(total.reshape(n_tp, share, shared + direct), 'tp', split_a...  10.5 us
    all_gather x1, waiting for transfers between devices, local(): lax.all_gather(packed, 'ep', axis=0, tiled=True, axis_index_groups=along_z)  8.26 us
    all_to_all x1, starting transfers between devices, local(): lax.all_to_all(total.reshape(n_tp, share, shared + direct), 'tp', split_a...  6.63 us
  transfers between devices with their start and end apart: 12, of which 7 were waited for; matrix products, arithmetic and copies ran while one was open for 3% of the time, Pallas kernels for 14%

profile of v3, /device:TPU:32, one launch (start us, length us, event | category | flops | bytes accessed | tf_op | source)
XLA Modules:
  0.0 177.8 jit_solution(1535531253879555874)
XLA Ops:
  6.5 3.0 %shard_map.128 = (bf16[512,896]{1,0:T(8,128)(2,1)}, bf16[512,256]{1,0:T(8,128)(2,1)}) custom-call(bf16[192,2048]{1,0:T(8,128)(2,1)} %rows_ref.4, f32[1,2048]{1,0:T(1,128)} %bitcast.24, s32[8,192]{1,0:T(8,128)} %bitcast.26), custom_call_target="tpu_custom_call" | custom-call | flops 226492416 | bytes 1980416 | tf_op jit(solution)/shard_map/pallas_call | solution.py:34
  9.6 9.7 %all-to-all-start = ((bf16[32,16,896]{2,1,0:T(8,128)(2,1)}), bf16[32,16,896]{2,1,0:T(8,128)(2,1)S(1)}, u32[]{:S(2)}, u32[]{:S(2)}) async-start(bf16[32,16,896]{2,1,0:T(8,128)(2,1)} %bitcast.21), calls=%async_computation | async-start | bytes 1835008 | tf_op jit(solution)/shard_map/all_to_all | solution.py:307
  19.2 0.0 all-gather.2.cloned.1.call-start
  19.3 0.7 constant_dynamic-slice_fusion.1
  20.0 0.0 copy-done.9
  20.0 0.0 copy-done.8
  20.0 0.7 pad_maximum_fusion
  20.7 0.0 all-gather.2.cloned.1.call-update
  20.8 27.2 %all-to-all-done = bf16[32,16,896]{2,1,0:T(8,128)(2,1)S(1)} async-done(((bf16[32,16,896]{2,1,0:T(8,128)(2,1)}), bf16[32,16,896]{2,1,0:T(8,128)(2,1)S(1)}, u32[]{:S(2)}, u32[]{:S(2)}) %all-to-all-start) | async-done | bytes 917536 | tf_op jit(solution)/shard_map/all_to_all | solution.py:307
  48.0 1.6 collective-permute-start
  49.6 3.9 %all-to-all-start.1 = ((bf16[32,16,256]{2,1,0:T(8,128)(2,1)}), bf16[32,16,256]{2,1,0:T(8,128)(2,1)S(1)}, u32[]{:S(2)}, u32[]{:S(2)}) async-start(bf16[32,16,256]{2,1,0:T(8,128)(2,1)} %bitcast.4), calls=%async_computation.1 | async-start | bytes 524288 | tf_op jit(solution)/shard_map/all_to_all | solution.py:307
  53.4 6.4 %shard_map.129.acc_ref = f32[512,1536]{1,0:T(8,128)} custom-call(bf16[512,896]{1,0:T(8,128)(2,1)} %bitcast.18, bf16[1,2048,1536]{2,1,0:T(8,128)(2,1)} %w_ref.3), custom_call_target="tpu_custom_call" | custom-call | flops 1409286144 | bytes 10354688 | tf_op jit(solution)/shard_map/pallas_call | solution.py:34
  59.9 8.3 %all-gather.2.cloned.1.call-done.near_ref = bf16[512,1280]{1,0:T(8,128)(2,1)} async-done(((bf16[64,1280]{1,0:T(8,128)(2,1)}), bf16[512,1280]{1,0:T(8,128)(2,1)}) %all-gather.2.cloned.1.call-update) | async-done | bytes 1310736 | tf_op jit(solution)/shard_map/all_gather | solution.py:304
  68.1 1.5 collective-permute-start.2
  69.6 0.0 all-to-all-done.1
  69.6 0.0 collective-permute-done.got_ref
  69.6 0.7 copy-done.5
  70.3 0.3 copy-done.6
  70.6 7.5 %shard_map.130 = (bf16[512,512]{1,0:T(8,128)(2,1)}, bf16[512,768]{1,0:T(8,128)(2,1)}, bf16[512,768]{1,0:T(8,128)(2,1)}) custom-call(f32[512,1536]{1,0:T(8,128)} %shard_map.129.acc_ref, bf16[512,896]{1,0:T(8,128)(2,1)} %copy-done.6, bf16[512,256]{1,0:T(8,128)(2,1)} %bitcast.20, bf16[1,2048,1536]{2,1,0:T(8,128)(2,1)} %w_ref.3, bf16[1,768,2048]{2,1,0:T(8,128)(2,1)} %down_ref.1, ...), custom_call_target="tpu_custom_call" | custom-call | flops 3422552064 | bytes 17170432 | tf_op jit(solution)/shard_map/pallas_call | solution.py:34
  78.2 1.3 collective-permute-start.1
  79.5 5.7 %all-to-all-start.3 = ((bf16[32,16,512]{2,1,0:T(8,128)(2,1)}), bf16[32,16,512]{2,1,0:T(8,128)(2,1)S(1)}, u32[]{:S(2)}, u32[]{:S(2)}) async-start(bf16[32,16,512]{2,1,0:T(8,128)(2,1)} %bitcast.22), calls=%async_computation.3 | async-start | bytes 1048576 | tf_op jit(solution)/shard_map/all_to_all | solution.py:307
  85.1 0.2 collective-permute-start.3
  85.4 11.1 %collective-permute-done.1 = bf16[512,768]{1,0:T(8,128)(2,1)} collective-permute-done((bf16[512,768]{1,0:T(8,128)(2,1)}, bf16[512,768]{1,0:T(8,128)(2,1)}, u32[]{:S(2)}, u32[]{:S(2)}) %collective-permute-start.1) | collective-permute-done | bytes 786464 | tf_op jit(solution)/shard_map/ppermute | solution.py:310
  96.5 2.2 %add_convert_fusion.after_ref = bf16[512,768]{1,0:T(8,128)(2,1)} fusion(bf16[512,768]{1,0:T(8,128)(2,1)} %collective-permute-done.1, bf16[512,768]{1,0:T(8,128)(2,1)S(1)} %copy-done.7), kind=kLoop, calls=%fused_computation | loop fusion | flops 1572864 | bytes 2359296 | tf_op jit(solution)/shard_map/convert_element_type | solution.py:369
  98.7 1.7 collective-permute-done.2.value_ref
  100.4 0.0 collective-permute-start.4
  100.4 2.5 %all-to-all-done.3 = bf16[32,16,512]{2,1,0:T(8,128)(2,1)S(1)} async-done(((bf16[32,16,512]{2,1,0:T(8,128)(2,1)}), bf16[32,16,512]{2,1,0:T(8,128)(2,1)S(1)}, u32[]{:S(2)}, u32[]{:S(2)}) %all-to-all-start.3) | async-done | bytes 524320 | tf_op jit(solution)/shard_map/all_to_all | solution.py:307
  102.9 6.3 %all-to-all-start.2 = ((bf16[32,16,768]{2,1,0:T(8,128)(2,1)}), bf16[32,16,768]{2,1,0:T(8,128)(2,1)S(1)}, u32[]{:S(2)}, u32[]{:S(2)}) async-start(bf16[32,16,768]{2,1,0:T(8,128)(2,1)} %bitcast.6), calls=%async_computation.2 | async-start | bytes 1572864 | tf_op jit(solution)/shard_map/all_to_all | solution.py:307
  109.2 0.4 fusion.3
  109.6 0.8 pad_maximum_fusion.1
  110.4 0.0 collective-permute-done.3.other_near_ref
  110.4 0.0 collective-permute-done.4.other_across_ref
  110.4 0.0 copy-done
  110.4 7.4 %shard_map.132 = (bf16[192,768]{1,0:T(8,128)(2,1)}, f32[192,768]{1,0:T(8,128)}, f32[192,512]{1,0:T(8,128)}) custom-call(bf16[192,2048]{1,0:T(8,128)(2,1)} %rows_ref.5, f32[1,2048]{1,0:T(1,128)} %bitcast.23, bf16[512,1280]{1,0:T(8,128)(2,1)} %all-gather.2.cloned.1.call-done.near_ref, bf16[512,1280]{1,0:T(8,128)(2,1)} %copy-done, ...), custom_call_target="tpu_custom_call" | custom-call | tf_op jit(solution)/shard_map/pallas_call | solution.py:34
  117.8 0.9 collective-permute-start.5
  118.7 3.1 %shard_map.127.map_ref = bf16[192,512]{1,0:T(8,128)(2,1)} custom-call(bf16[192,2048]{1,0:T(8,128)(2,1)} %rows_ref.4, f32[1,2048]{1,0:T(1,128)} %bitcast.25, bf16[128,2048]{1,0:T(8,128)(2,1)} %router_ref.1, s32[8,192]{1,0:T(8,128)} %bitcast.27), custom_call_target="tpu_custom_call" | custom-call | tf_op jit(solution)/shard_map/pallas_call | solution.py:34
  121.8 10.8 %all-to-all-done.2 = bf16[32,16,768]{2,1,0:T(8,128)(2,1)S(1)} async-done(((bf16[32,16,768]{2,1,0:T(8,128)(2,1)}), bf16[32,16,768]{2,1,0:T(8,128)(2,1)S(1)}, u32[]{:S(2)}, u32[]{:S(2)}) %all-to-all-start.2) | async-done | bytes 786464 | tf_op jit(solution)/shard_map/all_to_all | solution.py:307
  132.5 0.0 collective-permute-done.5.got_ref
  132.6 0.0 copy-start.1
  132.6 0.9 copy-done.1
  133.5 1.2 shard_map.133
  134.7 6.6 %all-to-all-start.4 = ((bf16[8,24,1280]{2,1,0:T(8,128)(2,1)}), bf16[8,24,1280]{2,1,0:T(8,128)(2,1)S(1)}, u32[]{:S(2)}, u32[]{:S(2)}) async-start(bf16[8,24,1280]{2,1,0:T(8,128)(2,1)} %bitcast.13), calls=%async_computation.4 | async-start | bytes 983040 | tf_op jit(solution)/shard_map/all_to_all | solution.py:422
  141.3 10.5 %all-to-all-done.4 = bf16[8,24,1280]{2,1,0:T(8,128)(2,1)S(1)} async-done(((bf16[8,24,1280]{2,1,0:T(8,128)(2,1)}), bf16[8,24,1280]{2,1,0:T(8,128)(2,1)S(1)}, u32[]{:S(2)}, u32[]{:S(2)}) %all-to-all-start.4) | async-done | bytes 491552 | tf_op jit(solution)/shard_map/all_to_all | solution.py:422
  151.9 0.1 convert_element_type.22
  152.0 0.9 fusion
  152.9 0.1 broadcast_in_dim.24
  153.0 17.0 %all_to_all.54 = bf16[8,24,2048]{2,1,0:T(8,128)(2,1)S(1)} all-to-all(bf16[8,24,2048]{2,1,0:T(8,128)(2,1)S(1)} %broadcast_in_dim.24), channel_id=1, replica_groups=mesh['ep'=32,'tp'=8] {'tp'}, dimensions={0} | all-to-all | bytes 1572864 | tf_op jit(solution)/shard_map/all_to_all | solution.py:434
  170.0 0.9 copy.17
  (17 shorter events, 0.1 us)
Async XLA Ops:
  6.5 13.5 %copy-start.9 = (bf16[64,512]{1,0:T(8,128)(2,1)S(1)}, bf16[64,512]{1,0:T(8,128)(2,1)}, u32[]{:S(2)}) copy-start(bf16[64,512]{1,0:T(8,128)(2,1)} %param.17) | copy-start | bytes 196612
  6.5 13.5 %copy-start.8 = (bf16[64,512]{1,0:T(8,128)(2,1)S(1)}, bf16[64,512]{1,0:T(8,128)(2,1)}, u32[]{:S(2)}) copy-start(bf16[64,512]{1,0:T(8,128)(2,1)} %param.19) | copy-start | bytes 196612
  9.6 38.4 %all-to-all-start = ((bf16[32,16,896]{2,1,0:T(8,128)(2,1)}), bf16[32,16,896]{2,1,0:T(8,128)(2,1)S(1)}, u32[]{:S(2)}, u32[]{:S(2)}) async-start(bf16[32,16,896]{2,1,0:T(8,128)(2,1)} %bitcast.21), calls=%async_computation | async-start | bytes 1835008 | tf_op jit(solution)/shard_map/all_to_all | solution.py:307
  19.2 48.9 %all-gather.2.cloned.1.call-start = ((), (), s32[]{:S(2)}) async-start(), calls=%async_computation.6 | async-start | bytes 1474560 | tf_op jit(solution)/shard_map/all_gather | solution.py:304
  48.0 5.4 %copy-start.4 = (bf16[32,16,896]{2,1,0:T(8,128)(2,1)}, bf16[32,16,896]{2,1,0:T(8,128)(2,1)S(1)}, u32[]{:S(2)}) copy-start(bf16[32,16,896]{2,1,0:T(8,128)(2,1)S(1)} %all-to-all-done) | copy-start | bytes 2752516
  48.0 21.6 %collective-permute-start = (bf16[512,896]{1,0:T(8,128)(2,1)S(1)}, bf16[512,896]{1,0:T(8,128)(2,1)S(1)}, u32[]{:S(2)}, u32[]{:S(2)}) collective-permute-start(bf16[512,896]{1,0:T(8,128)(2,1)S(1)} %bitcast.17), channel_id=1, source_target_pairs={{0,1},{1,0},{2,3},{3,2},{4,5},{5,4},{6,7},{7,6},{8,9},{9,8},{10,11... | collective-permute-start | bytes 2752520 | tf_op jit(solution)/shard_map/ppermute | solution.py:310
  49.6 20.0 %all-to-all-start.1 = ((bf16[32,16,256]{2,1,0:T(8,128)(2,1)}), bf16[32,16,256]{2,1,0:T(8,128)(2,1)S(1)}, u32[]{:S(2)}, u32[]{:S(2)}) async-start(bf16[32,16,256]{2,1,0:T(8,128)(2,1)} %bitcast.4), calls=%async_computation.1 | async-start | bytes 524288 | tf_op jit(solution)/shard_map/all_to_all | solution.py:307
  68.1 32.3 %collective-permute-start.2 = (bf16[512,1280]{1,0:T(8,128)(2,1)}, bf16[512,1280]{1,0:T(8,128)(2,1)S(1)}, u32[]{:S(2)}, u32[]{:S(2)}) collective-permute-start(bf16[512,1280]{1,0:T(8,128)(2,1)} %all-gather.2.cloned.1.call-done.near_ref), channel_id=1, source_target_pairs={{0,128},{8,136},{16,144},{24,152},{32,160},{40,168},{48,176},{56,1... | collective-permute-start | bytes 3932168 | tf_op jit(solution)/shard_map/ppermute | solution.py:364
  69.6 0.7 copy-start.5
  69.6 1.1 copy-start.6
  78.1 18.4 %copy-start.7 = (bf16[512,768]{1,0:T(8,128)(2,1)S(1)}, bf16[512,768]{1,0:T(8,128)(2,1)}, u32[]{:S(2)}) copy-start(bf16[512,768]{1,0:T(8,128)(2,1)} %get-tuple-element.15) | copy-start | bytes 2359300
  78.2 18.4 %collective-permute-start.1 = (bf16[512,768]{1,0:T(8,128)(2,1)}, bf16[512,768]{1,0:T(8,128)(2,1)}, u32[]{:S(2)}, u32[]{:S(2)}) collective-permute-start(bf16[512,768]{1,0:T(8,128)(2,1)} %get-tuple-element.16), channel_id=1, source_target_pairs={{0,1},{1,0},{2,3},{3,2},{4,5},{5,4},{6,7},{7,6},{8,9},{9,8},{10,11... | collective-permute-start | bytes 2359304 | tf_op jit(solution)/shard_map/ppermute | solution.py:310
  79.5 23.4 %all-to-all-start.3 = ((bf16[32,16,512]{2,1,0:T(8,128)(2,1)}), bf16[32,16,512]{2,1,0:T(8,128)(2,1)S(1)}, u32[]{:S(2)}, u32[]{:S(2)}) async-start(bf16[32,16,512]{2,1,0:T(8,128)(2,1)} %bitcast.22), calls=%async_computation.3 | async-start | bytes 1048576 | tf_op jit(solution)/shard_map/all_to_all | solution.py:307
  85.1 25.2 %collective-permute-start.3 = (bf16[512,1280]{1,0:T(8,128)(2,1)}, bf16[512,1280]{1,0:T(8,128)(2,1)}, u32[]{:S(2)}, u32[]{:S(2)}) collective-permute-start(bf16[512,1280]{1,0:T(8,128)(2,1)} %all-gather.2.cloned.1.call-done.near_ref), channel_id=1, source_target_pairs={{0,8},{8,0},{16,24},{24,16},{32,40},{40,32},{48,56},{56,48},{64,72... | collective-permute-start | bytes 3932168 | tf_op jit(solution)/shard_map/ppermute | solution.py:366
  100.4 10.0 %copy-start = (bf16[512,1280]{1,0:T(8,128)(2,1)}, bf16[512,1280]{1,0:T(8,128)(2,1)S(1)}, u32[]{:S(2)}) copy-start(bf16[512,1280]{1,0:T(8,128)(2,1)S(1)} %shard_map.131.across_ref) | copy-start | bytes 3932164
  100.4 10.0 %collective-permute-start.4 = (bf16[512,1280]{1,0:T(8,128)(2,1)S(1)}, bf16[512,1280]{1,0:T(8,128)(2,1)}, u32[]{:S(2)}, u32[]{:S(2)}) collective-permute-start(bf16[512,1280]{1,0:T(8,128)(2,1)S(1)} %shard_map.131.across_ref), channel_id=1, source_target_pairs={{0,8},{8,0},{16,24},{24,16},{32,40},{40,32},{48,56},{56,48},{64,72... | collective-permute-start | bytes 3932168 | tf_op jit(solution)/shard_map/ppermute | solution.py:382
  102.9 29.6 %all-to-all-start.2 = ((bf16[32,16,768]{2,1,0:T(8,128)(2,1)}), bf16[32,16,768]{2,1,0:T(8,128)(2,1)S(1)}, u32[]{:S(2)}, u32[]{:S(2)}) async-start(bf16[32,16,768]{2,1,0:T(8,128)(2,1)} %bitcast.6), calls=%async_computation.2 | async-start | bytes 1572864 | tf_op jit(solution)/shard_map/all_to_all | solution.py:307
  117.8 14.8 %copy-start.2 = (f32[192,768]{1,0:T(8,128)S(1)}, f32[192,768]{1,0:T(8,128)}, u32[]{:S(2)}) copy-start(f32[192,768]{1,0:T(8,128)} %get-tuple-element.18.kept_ref) | copy-start | bytes 1769476
  117.8 14.8 %copy-start.3 = (f32[192,512]{1,0:T(8,128)S(1)}, f32[192,512]{1,0:T(8,128)}, u32[]{:S(2)}) copy-start(f32[192,512]{1,0:T(8,128)} %get-tuple-element.20.direct_ref) | copy-start | bytes 1179652
  117.8 14.8 %collective-permute-start.5 = (bf16[192,768]{1,0:T(8,128)(2,1)}, bf16[192,768]{1,0:T(8,128)(2,1)S(1)}, u32[]{:S(2)}, u32[]{:S(2)}) collective-permute-start(bf16[192,768]{1,0:T(8,128)(2,1)} %get-tuple-element.19), channel_id=1, source_target_pairs={{0,1},{1,0},{2,3},{3,2},{4,5},{5,4},{6,7},{7,6},{8,9},{9,8},{10,11... | collective-permute-start | bytes 884744 | tf_op jit(solution)/shard_map/ppermute | solution.py:310
  132.6 0.9 copy-start.1
  134.7 17.2 %all-to-all-start.4 = ((bf16[8,24,1280]{2,1,0:T(8,128)(2,1)}), bf16[8,24,1280]{2,1,0:T(8,128)(2,1)S(1)}, u32[]{:S(2)}, u32[]{:S(2)}) async-start(bf16[8,24,1280]{2,1,0:T(8,128)(2,1)} %bitcast.13), calls=%async_computation.4 | async-start | bytes 983040 | tf_op jit(solution)/shard_map/all_to_all | solution.py:422
Sparse Core Ops, SparseCore 0:
  21.8 46.2 all-gather.1

commit v4 on v3

--- a/solution.py
+++ b/solution.py
@@ -121,15 +121,13 @@
     near_ref,
     direct_ref,
     handed_ref,
-    kept_ref,
+    hidden_ref,
     acc,
-    x_buf,
     w_buf,
     w_down,
     hidden,
     out_direct,
     out_handed,
-    out_kept,
     sems,
 ):
     side = lax.axis_index("tp") % 2
@@ -144,7 +142,7 @@
     other = pl.multiple_of((1 - side) * width, width)
     ff = hidden.shape[1]
     tile = 256
-    inputs = [started(got_ref, x_buf.at[:, :width]), started(both_ref, x_buf.at[:, width:])]
+    split = width
     strips = []
     for at in range(0, ff, tile):
         strip = []
@@ -156,37 +154,50 @@
                 started(acc_ref.at[:, columns], acc.at[:, columns]),
             ]
         strips.append(strip)
-    last = started(down_ref.at[0], w_down)
-    for copy in inputs:
-        copy.wait()
-    x = x_buf[...]
+    width = out_handed.shape[1]
+    partner = pl.multiple_of((1 - side) * width, width)
+    last = [
+        started(down_ref.at[0, :, pl.ds(partner, width)], w_down.at[:, :width]),
+        started(down_ref.at[0, :, 2 * width :], w_down.at[:, width:]),
+    ]
+
+    def product(columns):
+        got = jnp.dot(got_ref[...], w_buf[:split, columns], preferred_element_type=F32)
+        both = jnp.dot(both_ref[...], w_buf[split:, columns], preferred_element_type=F32)
+        return acc[:, columns] + got + both
+
     for step, strip in enumerate(strips):
         for copy in strip:
             copy.wait()
         at = step * tile
-        gate = acc[:, at : at + tile] + jnp.dot(
-            x, w_buf[:, at : at + tile], preferred_element_type=F32
-        )
-        up = acc[:, ff + at : ff + at + tile] + jnp.dot(
-            x, w_buf[:, ff + at : ff + at + tile], preferred_element_type=F32
-        )
+        gate = product(slice(at, at + tile))
+        up = product(slice(ff + at, ff + at + tile))
         hidden[:, at : at + tile] = (jax.nn.silu(gate) * up).astype(BF16)
-    last.wait()
-    width = out_kept.shape[1]
-    mine = pl.multiple_of(side * width, width)
-    other = pl.multiple_of((1 - side) * width, width)
+    back = [started(hidden, hidden_ref)]
+    for copy in last:
+        copy.wait()
 
     def projected(columns):
         return jnp.dot(hidden[...], w_down[:, columns], preferred_element_type=F32).astype(BF16)
 
-    out_handed[...] = projected(pl.ds(other, width))
-    back = [started(out_handed, handed_ref)]
-    out_direct[...] = projected(pl.ds(2 * width, out_direct.shape[1]))
+    width = out_handed.shape[1]
+    out_handed[...] = projected(pl.ds(0, width))
+    back.append(started(out_handed, handed_ref))
+    out_direct[...] = projected(pl.ds(width, out_direct.shape[1]))
     back.append(started(out_direct, direct_ref))
-    out_kept[...] = projected(pl.ds(mine, width))
-    back.append(started(out_kept, kept_ref))
     for copy in back:
         copy.wait()
+
+
+def kept_body(hidden_ref, down_ref, out_ref, w_down, sem):
+    width = out_ref.shape[1]
+    mine = pl.multiple_of(lax.axis_index("tp") % 2 * width, width)
+    copy = pltpu.make_async_copy(down_ref.at[0, :, pl.ds(mine, width)], w_down, sem)
+    copy.start()
+    copy.wait()
+    out_ref[...] = jnp.dot(
+        hidden_ref[...], w_down[...], preferred_element_type=F32
+    ).astype(BF16)
 
 
 def attention_body(
@@ -259,7 +270,9 @@
     )
 
 
-def combine_body(map_ref, shared_ref, both_ref, kept_ref, got_ref, direct_ref, out_ref):
+def combine_body(
+    map_ref, shared_ref, both_ref, kept_ref, got_ref, direct_ref, own_ref, out_ref, own_out_ref
+):
     width = kept_ref.shape[1]
     shared = jnp.dot(map_ref[...], shared_ref[...], preferred_element_type=F32)
     out_ref[:, :width] = (shared + kept_ref[...] + got_ref[...].astype(F32)).astype(BF16)
@@ -338,28 +351,36 @@
         specs=[vmem(), anywhere()],
         scratch=[pltpu.VMEM((shared_in, ff2), BF16), pltpu.SemaphoreType.DMA],
     )
-    out_both, handed, kept = call(
+    out_both, handed, hidden = call(
         expert_body,
         [
             jax.ShapeDtypeStruct((places, direct), BF16),
             jax.ShapeDtypeStruct((places, shared), BF16),
-            jax.ShapeDtypeStruct((places, shared), BF16),
+            jax.ShapeDtypeStruct((places, ff), BF16),
         ],
         (acc, received, arrived_both, gate_up_weight, down_weight, near),
         2 * places * (shared_in + direct_in) * ff2 + 2 * places * ff * d_model,
-        specs=[anywhere()] * 6,
+        limit=52,
+        specs=[anywhere(), vmem(), vmem()] + [anywhere()] * 3,
         out_specs=[anywhere()] * 3,
         scratch=[
             pltpu.VMEM((places, ff2), F32),
-            pltpu.VMEM((places, shared_in + direct_in), BF16),
             pltpu.VMEM((shared_in + direct_in, ff2), BF16),
-            pltpu.VMEM((ff, d_model), BF16),
+            pltpu.VMEM((ff, shared + direct), BF16),
             pltpu.VMEM((places, ff), BF16),
             pltpu.VMEM((places, direct), BF16),
             pltpu.VMEM((places, shared), BF16),
-            pltpu.VMEM((places, shared), BF16),
             pltpu.SemaphoreType.DMA((32,)),
         ],
+    )
+    (kept,) = call(
+        kept_body,
+        [jax.ShapeDtypeStruct((places, shared), BF16)],
+        (hidden, down_weight),
+        0,
+        cost=0,
+        specs=[vmem(), anywhere()],
+        scratch=[pltpu.VMEM((ff, shared), BF16), pltpu.SemaphoreType.DMA],
     )
     across = lax.ppermute(near, "ep", [(i, i ^ 16) for i in range(n_ep)])
     cores = [(i, i ^ 1) for i in range(n_ep)]
@@ -411,14 +432,21 @@
         scratch=[pltpu.VMEM((d_model, packed.shape[1]), BF16)],
     )
     att_got = swapped(att_handed)
-    (total,) = call(
+    share = rows // n_tp
+    own = lax.dynamic_slice_in_dim(residual_in, rank * share, share, 0)
+    total, own = call(
         combine_body,
-        [jax.ShapeDtypeStruct((rows, shared + direct), BF16)],
-        (combine, returned, returned_both, att_kept, att_got, att_both),
+        [
+            jax.ShapeDtypeStruct((rows, shared + direct), BF16),
+            jax.ShapeDtypeStruct(own.shape, BF16),
+        ],
+        (combine, returned, returned_both, att_kept, att_got, att_both, own),
         2 * rows * places * (shared + direct),
         limit=16,
-    )
-    share = rows // n_tp
+        specs=[vmem()] * 6 + [anywhere()],
+        out_specs=[vmem(), anywhere()],
+        aliases={6: 1},
+    )
     terms = lax.all_to_all(
         total.reshape(n_tp, share, shared + direct),
         "tp",
@@ -429,7 +457,6 @@
     terms = terms.astype(F32)
     sums = [jnp.sum(terms[h::2, :, :shared], 0) for h in range(2)]
     sums = jnp.concatenate(sums + [jnp.sum(terms[:, :, shared:], 0)], 1)
-    own = lax.dynamic_slice_in_dim(residual_in, rank * share, share, 0)
     mine = (own.astype(F32) + sums).astype(BF16)
     everyone = lax.all_to_all(
         jnp.broadcast_to(mine[None], (n_tp, share, d_model)),

time: 179 us -> 176 us (0.983)
  blocking collectives: 17 us -> 33 us
  waiting for transfers between devices: 72.2 us -> 56.4 us
  starting transfers between devices: 37.6 us -> 31.3 us
  Pallas kernels: 28.6 us -> 32.7 us
    all_to_all x0 -> x1, blocking collectives: none -> 17.3 us  [local(): lax.all_to_all(total.reshape(n_tp, share, shared + direct), 'tp', split_a...]
    all_to_all x1 -> x0, waiting for transfers between devices: 10.5 us -> none  [local(): lax.all_to_all(total.reshape(n_tp, share, shared + direct), 'tp', split_a...]
    all_to_all x1 -> x0, starting transfers between devices: 6.63 us -> none  [local(): lax.all_to_all(total.reshape(n_tp, share, shared + direct), 'tp', split_a...]
    ppermute x3, waiting for transfers between devices: 11.1 us -> 6.83 us  [swapped(): return lax.ppermute(value, 'tp', partner)]
    pallas_call x7 -> x8, Pallas kernels: 28.6 us -> 32.7 us  [call(): pl.pallas_call(body, out_shape=out_shape, in_specs=specs or [vmem()] * le...]
  transfers between devices with their start and end apart: 12 -> 11, of which waited for: 7 -> 6; matrix products, arithmetic and copies ran while one was open for 3% -> 3% of each run, Pallas kernels for 14% -> 17%
where the time goes in v4:
time: 176 us; the launch traced here: 175 us
  waiting for transfers between devices  56.4 us (32%)
  blocking collectives  33 us (19%)
  Pallas kernels  32.7 us (19%)
  starting transfers between devices  31.3 us (18%)
  between operations  13.6 us (8%)
  other arithmetic  4.49 us (3%)
  local copies, waits for them, and re-layouts  3.54 us (2%)
    all_to_all x4, waiting for transfers between devices, to_owners(): return lax.all_to_all(value, 'ep', split_axis=0, concat_axis=0, tiled=True)  39.2 us
    pallas_call x8, Pallas kernels, call(): pl.pallas_call(body, out_shape=out_shape, in_specs=specs or [vmem()] * le...  32.7 us
    all_to_all x4, starting transfers between devices, to_owners(): return lax.all_to_all(value, 'ep', split_axis=0, concat_axis=0, tiled=True)  25.8 us
    all_to_all x1, blocking collectives, local(): lax.all_to_all(total.reshape(n_tp, share, shared + direct), 'tp', split_a...  17.3 us
    all_to_all x1, blocking collectives, local(): lax.all_to_all(jnp.broadcast_to(mine[None], (n_tp, share, d_model)), 'tp'...  15.7 us
    all_gather x1, waiting for transfers between devices, local(): lax.all_gather(packed, 'ep', axis=0, tiled=True, axis_index_groups=along_z)  8.23 us
    ppermute x3, waiting for transfers between devices, swapped(): return lax.ppermute(value, 'tp', partner)  6.83 us
    ppermute x3, starting transfers between devices, swapped(): return lax.ppermute(value, 'tp', partner)  3.8 us
  transfers between devices with their start and end apart: 11, of which 6 were waited for; matrix products, arithmetic and copies ran while one was open for 3% of the time, Pallas kernels for 17%

profile of v4, /device:TPU:32, one launch (start us, length us, event | category | flops | bytes accessed | tf_op | source)
XLA Modules:
  0.0 174.9 jit_solution(14869568405645849741)
XLA Ops:
  6.5 3.0 %shard_map.128 = (bf16[512,896]{1,0:T(8,128)(2,1)}, bf16[512,256]{1,0:T(8,128)(2,1)}) custom-call(bf16[192,2048]{1,0:T(8,128)(2,1)} %rows_ref.4, f32[1,2048]{1,0:T(1,128)} %bitcast.24, s32[8,192]{1,0:T(8,128)} %bitcast.26), custom_call_target="tpu_custom_call" | custom-call | flops 226492416 | bytes 1980416 | tf_op jit(solution)/shard_map/pallas_call | solution.py:34
  9.6 9.7 %all-to-all-start = ((bf16[32,16,896]{2,1,0:T(8,128)(2,1)}), bf16[32,16,896]{2,1,0:T(8,128)(2,1)S(1)}, u32[]{:S(2)}, u32[]{:S(2)}) async-start(bf16[32,16,896]{2,1,0:T(8,128)(2,1)} %bitcast.22), calls=%async_computation | async-start | bytes 1835008 | tf_op jit(solution)/shard_map/all_to_all | solution.py:320
  19.2 0.0 all-gather.2.cloned.1.call-start
  19.3 0.7 constant_dynamic-slice_fusion.2
  20.0 0.0 copy-done.6
  20.0 0.0 copy-done.5
  20.0 0.7 pad_maximum_fusion
  20.7 0.0 all-gather.2.cloned.1.call-update
  20.8 27.2 %all-to-all-done = bf16[32,16,896]{2,1,0:T(8,128)(2,1)S(1)} async-done(((bf16[32,16,896]{2,1,0:T(8,128)(2,1)}), bf16[32,16,896]{2,1,0:T(8,128)(2,1)S(1)}, u32[]{:S(2)}, u32[]{:S(2)}) %all-to-all-start) | async-done | bytes 917536 | tf_op jit(solution)/shard_map/all_to_all | solution.py:320
  48.0 1.6 collective-permute-start
  49.6 3.9 %all-to-all-start.1 = ((bf16[32,16,256]{2,1,0:T(8,128)(2,1)}), bf16[32,16,256]{2,1,0:T(8,128)(2,1)S(1)}, u32[]{:S(2)}, u32[]{:S(2)}) async-start(bf16[32,16,256]{2,1,0:T(8,128)(2,1)} %bitcast.4), calls=%async_computation.1 | async-start | bytes 524288 | tf_op jit(solution)/shard_map/all_to_all | solution.py:320
  53.4 0.0 copy-done.4
  53.4 6.4 %shard_map.129.acc_ref = f32[512,1536]{1,0:T(8,128)} custom-call(bf16[512,896]{1,0:T(8,128)(2,1)} %bitcast.20, bf16[1,2048,1536]{2,1,0:T(8,128)(2,1)} %w_ref.3), custom_call_target="tpu_custom_call" | custom-call | flops 1409286144 | bytes 10354688 | tf_op jit(solution)/shard_map/pallas_call | solution.py:34
  59.9 8.2 %all-gather.2.cloned.1.call-done.near_ref = bf16[512,1280]{1,0:T(8,128)(2,1)} async-done(((bf16[64,1280]{1,0:T(8,128)(2,1)}), bf16[512,1280]{1,0:T(8,128)(2,1)}) %all-gather.2.cloned.1.call-update) | async-done | bytes 1310736 | tf_op jit(solution)/shard_map/all_gather | solution.py:317
  68.1 1.5 collective-permute-start.2
  69.6 0.0 all-to-all-done.1
  69.6 0.0 collective-permute-done.got_ref
  69.6 8.2 %shard_map.130 = (bf16[512,512]{1,0:T(8,128)(2,1)}, bf16[512,768]{1,0:T(8,128)(2,1)S(1)}, bf16[512,768]{1,0:T(8,128)(2,1)}) custom-call(f32[512,1536]{1,0:T(8,128)} %shard_map.129.acc_ref, bf16[512,896]{1,0:T(8,128)(2,1)} %collective-permute-done.got_ref, bf16[512,256]{1,0:T(8,128)(2,1)S(1)} %bitcast.17, bf16[1,2048,1536]{2,1,0:T(8,128)(2,1)} %w_ref.3, ...), custom_call_target="tpu_custom_call" | custom-call | flops 3422552064 | bytes 17170432 | tf_op jit(solution)/shard_map/pallas_call | solution.py:34
  77.8 1.3 collective-permute-start.1
  79.2 5.7 %all-to-all-start.3 = ((bf16[32,16,512]{2,1,0:T(8,128)(2,1)}), bf16[32,16,512]{2,1,0:T(8,128)(2,1)S(1)}, u32[]{:S(2)}, u32[]{:S(2)}) async-start(bf16[32,16,512]{2,1,0:T(8,128)(2,1)} %bitcast.8), calls=%async_computation.3 | async-start | bytes 1048576 | tf_op jit(solution)/shard_map/all_to_all | solution.py:320
  84.8 0.2 collective-permute-start.3
  85.1 4.1 %shard_map.131 = bf16[512,768]{1,0:T(8,128)(2,1)} custom-call(bf16[512,768]{1,0:T(8,128)(2,1)} %get-tuple-element.17.hidden_ref, bf16[1,768,2048]{2,1,0:T(8,128)(2,1)} %down_ref.3), custom_call_target="tpu_custom_call" | custom-call | tf_op jit(solution)/shard_map/pallas_call | solution.py:34
  89.1 6.8 %collective-permute-done.1 = bf16[512,768]{1,0:T(8,128)(2,1)} collective-permute-done((bf16[512,768]{1,0:T(8,128)(2,1)S(1)}, bf16[512,768]{1,0:T(8,128)(2,1)}, u32[]{:S(2)}, u32[]{:S(2)}) %collective-permute-start.1) | collective-permute-done | bytes 786464 | tf_op jit(solution)/shard_map/ppermute | solution.py:323
  96.0 2.4 %add_convert_fusion.after_ref = bf16[512,768]{1,0:T(8,128)(2,1)} fusion(bf16[512,768]{1,0:T(8,128)(2,1)} %collective-permute-done.1, bf16[512,768]{1,0:T(8,128)(2,1)} %shard_map.131), kind=kLoop, calls=%fused_computation | loop fusion | flops 1572864 | bytes 2359296 | tf_op jit(solution)/shard_map/convert_element_type | solution.py:390
  98.4 2.1 %collective-permute-done.2.value_ref = bf16[512,1280]{1,0:T(8,128)(2,1)S(1)} collective-permute-done((bf16[512,1280]{1,0:T(8,128)(2,1)}, bf16[512,1280]{1,0:T(8,128)(2,1)S(1)}, u32[]{:S(2)}, u32[]{:S(2)}) %collective-permute-start.2) | collective-permute-done | bytes 1310752 | tf_op jit(solution)/shard_map/ppermute | solution.py:385
  100.5 0.0 collective-permute-start.4
  100.5 2.1 %all-to-all-done.3 = bf16[32,16,512]{2,1,0:T(8,128)(2,1)S(1)} async-done(((bf16[32,16,512]{2,1,0:T(8,128)(2,1)}), bf16[32,16,512]{2,1,0:T(8,128)(2,1)S(1)}, u32[]{:S(2)}, u32[]{:S(2)}) %all-to-all-start.3) | async-done | bytes 524320 | tf_op jit(solution)/shard_map/all_to_all | solution.py:320
  102.6 6.6 %all-to-all-start.2 = ((bf16[32,16,768]{2,1,0:T(8,128)(2,1)}), bf16[32,16,768]{2,1,0:T(8,128)(2,1)S(1)}, u32[]{:S(2)}, u32[]{:S(2)}) async-start(bf16[32,16,768]{2,1,0:T(8,128)(2,1)} %bitcast.6), calls=%async_computation.2 | async-start | bytes 1572864 | tf_op jit(solution)/shard_map/all_to_all | solution.py:320
  109.2 0.4 fusion.3
  109.6 0.8 pad_maximum_fusion.1
  110.4 0.0 collective-permute-done.3.other_near_ref
  110.4 0.0 collective-permute-done.4.other_across_ref
  110.4 0.0 copy-done
  110.4 7.4 %shard_map.133 = (bf16[192,768]{1,0:T(8,128)(2,1)}, f32[192,768]{1,0:T(8,128)}, f32[192,512]{1,0:T(8,128)}) custom-call(bf16[192,2048]{1,0:T(8,128)(2,1)} %rows_ref.5, f32[1,2048]{1,0:T(1,128)} %bitcast.23, bf16[512,1280]{1,0:T(8,128)(2,1)} %all-gather.2.cloned.1.call-done.near_ref, bf16[512,1280]{1,0:T(8,128)(2,1)} %copy-done, ...), custom_call_target="tpu_custom_call" | custom-call | tf_op jit(solution)/shard_map/pallas_call | solution.py:34
  117.8 0.9 collective-permute-start.5
  118.7 3.1 %shard_map.127.map_ref = bf16[192,512]{1,0:T(8,128)(2,1)} custom-call(bf16[192,2048]{1,0:T(8,128)(2,1)} %rows_ref.4, f32[1,2048]{1,0:T(1,128)} %bitcast.25, bf16[128,2048]{1,0:T(8,128)(2,1)} %router_ref.1, s32[8,192]{1,0:T(8,128)} %bitcast.27), custom_call_target="tpu_custom_call" | custom-call | tf_op jit(solution)/shard_map/pallas_call | solution.py:34
  121.8 0.9 constant_dynamic-slice_fusion.own_ref
  122.7 9.9 %all-to-all-done.2 = bf16[32,16,768]{2,1,0:T(8,128)(2,1)S(1)} async-done(((bf16[32,16,768]{2,1,0:T(8,128)(2,1)}), bf16[32,16,768]{2,1,0:T(8,128)(2,1)S(1)}, u32[]{:S(2)}, u32[]{:S(2)}) %all-to-all-start.2) | async-done | bytes 786464 | tf_op jit(solution)/shard_map/all_to_all | solution.py:320
  132.5 0.0 collective-permute-done.5.got_ref
  132.6 0.0 copy-done.2
  132.6 0.0 copy-done.3
  132.6 0.9 copy-done.1
  133.5 0.4 shard_map.134
  133.9 17.3 %all_to_all.54 = bf16[8,24,1280]{2,1,0:T(8,128)(2,1)S(1)} all-to-all(bf16[8,24,1280]{2,1,0:T(8,128)(2,1)S(1)} %bitcast.18), channel_id=1, replica_groups=mesh['ep'=32,'tp'=8] {'tp'}, dimensions={0} | all-to-all | bytes 983040 | tf_op jit(solution)/shard_map/all_to_all | solution.py:450
  151.3 0.1 convert_element_type.22
  151.4 0.1 broadcast_in_dim.24
  151.5 15.7 %all_to_all.55 = bf16[8,24,2048]{2,1,0:T(8,128)(2,1)S(1)} all-to-all(bf16[8,24,2048]{2,1,0:T(8,128)(2,1)S(1)} %broadcast_in_dim.24), channel_id=1, replica_groups=mesh['ep'=32,'tp'=8] {'tp'}, dimensions={0} | all-to-all | bytes 1572864 | tf_op jit(solution)/shard_map/all_to_all | solution.py:461
  167.2 0.9 copy.19
  (12 shorter events, 0.1 us)
Async XLA Ops:
  6.5 13.5 %copy-start.6 = (bf16[64,512]{1,0:T(8,128)(2,1)S(1)}, bf16[64,512]{1,0:T(8,128)(2,1)}, u32[]{:S(2)}) copy-start(bf16[64,512]{1,0:T(8,128)(2,1)} %param.17) | copy-start | bytes 196612
  6.5 13.5 %copy-start.5 = (bf16[64,512]{1,0:T(8,128)(2,1)S(1)}, bf16[64,512]{1,0:T(8,128)(2,1)}, u32[]{:S(2)}) copy-start(bf16[64,512]{1,0:T(8,128)(2,1)} %param.19) | copy-start | bytes 196612
  9.6 38.4 %all-to-all-start = ((bf16[32,16,896]{2,1,0:T(8,128)(2,1)}), bf16[32,16,896]{2,1,0:T(8,128)(2,1)S(1)}, u32[]{:S(2)}, u32[]{:S(2)}) async-start(bf16[32,16,896]{2,1,0:T(8,128)(2,1)} %bitcast.22), calls=%async_computation | async-start | bytes 1835008 | tf_op jit(solution)/shard_map/all_to_all | solution.py:320
  19.2 48.9 %all-gather.2.cloned.1.call-start = ((), (), s32[]{:S(2)}) async-start(), calls=%async_computation.6 | async-start | bytes 1474560 | tf_op jit(solution)/shard_map/all_gather | solution.py:317
  48.0 5.4 %copy-start.4 = (bf16[32,16,896]{2,1,0:T(8,128)(2,1)}, bf16[32,16,896]{2,1,0:T(8,128)(2,1)S(1)}, u32[]{:S(2)}) copy-start(bf16[32,16,896]{2,1,0:T(8,128)(2,1)S(1)} %all-to-all-done) | copy-start | bytes 2752516
  48.0 21.6 %collective-permute-start = (bf16[512,896]{1,0:T(8,128)(2,1)S(1)}, bf16[512,896]{1,0:T(8,128)(2,1)}, u32[]{:S(2)}, u32[]{:S(2)}) collective-permute-start(bf16[512,896]{1,0:T(8,128)(2,1)S(1)} %bitcast.19), channel_id=1, source_target_pairs={{0,1},{1,0},{2,3},{3,2},{4,5},{5,4},{6,7},{7,6},{8,9},{9,8},{10,11... | collective-permute-start | bytes 2752520 | tf_op jit(solution)/shard_map/ppermute | solution.py:323
  49.6 20.0 %all-to-all-start.1 = ((bf16[32,16,256]{2,1,0:T(8,128)(2,1)}), bf16[32,16,256]{2,1,0:T(8,128)(2,1)S(1)}, u32[]{:S(2)}, u32[]{:S(2)}) async-start(bf16[32,16,256]{2,1,0:T(8,128)(2,1)} %bitcast.4), calls=%async_computation.1 | async-start | bytes 524288 | tf_op jit(solution)/shard_map/all_to_all | solution.py:320
  68.1 32.4 %collective-permute-start.2 = (bf16[512,1280]{1,0:T(8,128)(2,1)}, bf16[512,1280]{1,0:T(8,128)(2,1)S(1)}, u32[]{:S(2)}, u32[]{:S(2)}) collective-permute-start(bf16[512,1280]{1,0:T(8,128)(2,1)} %all-gather.2.cloned.1.call-done.near_ref), channel_id=1, source_target_pairs={{0,128},{8,136},{16,144},{24,152},{32,160},{40,168},{48,176},{56,1... | collective-permute-start | bytes 3932168 | tf_op jit(solution)/shard_map/ppermute | solution.py:385
  77.8 18.1 %collective-permute-start.1 = (bf16[512,768]{1,0:T(8,128)(2,1)S(1)}, bf16[512,768]{1,0:T(8,128)(2,1)}, u32[]{:S(2)}, u32[]{:S(2)}) collective-permute-start(bf16[512,768]{1,0:T(8,128)(2,1)S(1)} %get-tuple-element.18), channel_id=1, source_target_pairs={{0,1},{1,0},{2,3},{3,2},{4,5},{5,4},{6,7},{7,6},{8,9},{9,8},{10,11... | collective-permute-start | bytes 2359304 | tf_op jit(solution)/shard_map/ppermute | solution.py:323
  79.2 23.4 %all-to-all-start.3 = ((bf16[32,16,512]{2,1,0:T(8,128)(2,1)}), bf16[32,16,512]{2,1,0:T(8,128)(2,1)S(1)}, u32[]{:S(2)}, u32[]{:S(2)}) async-start(bf16[32,16,512]{2,1,0:T(8,128)(2,1)} %bitcast.8), calls=%async_computation.3 | async-start | bytes 1048576 | tf_op jit(solution)/shard_map/all_to_all | solution.py:320
  84.8 25.6 %collective-permute-start.3 = (bf16[512,1280]{1,0:T(8,128)(2,1)}, bf16[512,1280]{1,0:T(8,128)(2,1)}, u32[]{:S(2)}, u32[]{:S(2)}) collective-permute-start(bf16[512,1280]{1,0:T(8,128)(2,1)} %all-gather.2.cloned.1.call-done.near_ref), channel_id=1, source_target_pairs={{0,8},{8,0},{16,24},{24,16},{32,40},{40,32},{48,56},{56,48},{64,72... | collective-permute-start | bytes 3932168 | tf_op jit(solution)/shard_map/ppermute | solution.py:387
  100.5 10.0 %copy-start = (bf16[512,1280]{1,0:T(8,128)(2,1)}, bf16[512,1280]{1,0:T(8,128)(2,1)S(1)}, u32[]{:S(2)}) copy-start(bf16[512,1280]{1,0:T(8,128)(2,1)S(1)} %shard_map.132.across_ref) | copy-start | bytes 3932164
  100.5 10.0 %collective-permute-start.4 = (bf16[512,1280]{1,0:T(8,128)(2,1)S(1)}, bf16[512,1280]{1,0:T(8,128)(2,1)}, u32[]{:S(2)}, u32[]{:S(2)}) collective-permute-start(bf16[512,1280]{1,0:T(8,128)(2,1)S(1)} %shard_map.132.across_ref), channel_id=1, source_target_pairs={{0,8},{8,0},{16,24},{24,16},{32,40},{40,32},{48,56},{56,48},{64,72... | collective-permute-start | bytes 3932168 | tf_op jit(solution)/shard_map/ppermute | solution.py:403
  102.6 30.0 %all-to-all-start.2 = ((bf16[32,16,768]{2,1,0:T(8,128)(2,1)}), bf16[32,16,768]{2,1,0:T(8,128)(2,1)S(1)}, u32[]{:S(2)}, u32[]{:S(2)}) async-start(bf16[32,16,768]{2,1,0:T(8,128)(2,1)} %bitcast.6), calls=%async_computation.2 | async-start | bytes 1572864 | tf_op jit(solution)/shard_map/all_to_all | solution.py:320
  117.8 14.7 %copy-start.2 = (f32[192,768]{1,0:T(8,128)S(1)}, f32[192,768]{1,0:T(8,128)}, u32[]{:S(2)}) copy-start(f32[192,768]{1,0:T(8,128)} %get-tuple-element.20.kept_ref) | copy-start | bytes 1769476
  117.8 14.7 %copy-start.3 = (f32[192,512]{1,0:T(8,128)S(1)}, f32[192,512]{1,0:T(8,128)}, u32[]{:S(2)}) copy-start(f32[192,512]{1,0:T(8,128)} %get-tuple-element.22.direct_ref) | copy-start | bytes 1179652
  117.8 14.7 %collective-permute-start.5 = (bf16[192,768]{1,0:T(8,128)(2,1)}, bf16[192,768]{1,0:T(8,128)(2,1)S(1)}, u32[]{:S(2)}, u32[]{:S(2)}) collective-permute-start(bf16[192,768]{1,0:T(8,128)(2,1)} %get-tuple-element.21), channel_id=1, source_target_pairs={{0,1},{1,0},{2,3},{3,2},{4,5},{5,4},{6,7},{7,6},{8,9},{9,8},{10,11... | collective-permute-start | bytes 884744 | tf_op jit(solution)/shard_map/ppermute | solution.py:323
  132.6 0.9 copy-start.1
Sparse Core Ops, SparseCore 0:
  21.8 46.2 all-gather.1

commit v5 on v4

--- a/solution.py
+++ b/solution.py
@@ -342,6 +342,7 @@
         (shortcut, moe_gain, router_weight, ids),
         2 * rows * 128 * d_model,
         cost=0,
+        limit=24,
     )
     (acc,) = call(
         first_part_body,

time: 176 us -> 176 us (level)
  transfers between devices with their start and end apart: 11 -> 11, of which waited for: 6 -> 6; matrix products, arithmetic and copies ran while one was open for 3% -> 3% of each run, Pallas kernels for 17% -> 16%
where the time goes in v5:
time: 176 us; the launch traced here: 175 us
  waiting for transfers between devices  57.5 us (33%)
  blocking collectives  33 us (19%)
  Pallas kernels  31.7 us (18%)
  starting transfers between devices  31.2 us (18%)
  between operations  13.6 us (8%)
  other arithmetic  4.22 us (2%)
  local copies, waits for them, and re-layouts  3.68 us (2%)
    all_to_all x4, waiting for transfers between devices, to_owners(): return lax.all_to_all(value, 'ep', split_axis=0, concat_axis=0, tiled=True)  40.1 us
    pallas_call x8, Pallas kernels, call(): pl.pallas_call(body, out_shape=out_shape, in_specs=specs or [vmem()] * le...  31.7 us
    all_to_all x4, starting transfers between devices, to_owners(): return lax.all_to_all(value, 'ep', split_axis=0, concat_axis=0, tiled=True)  25.7 us
    all_to_all x1, blocking collectives, local(): lax.all_to_all(total.reshape(n_tp, share, shared + direct), 'tp', split_a...  17.3 us
    all_to_all x1, blocking collectives, local(): lax.all_to_all(jnp.broadcast_to(mine[None], (n_tp, share, d_model)), 'tp'...  15.7 us
    all_gather x1, waiting for transfers between devices, local(): lax.all_gather(packed, 'ep', axis=0, tiled=True, axis_index_groups=along_z)  8.23 us
    ppermute x3, waiting for transfers between devices, swapped(): return lax.ppermute(value, 'tp', partner)  6.72 us
    ppermute x3, starting transfers between devices, swapped(): return lax.ppermute(value, 'tp', partner)  3.71 us
  transfers between devices with their start and end apart: 11, of which 6 were waited for; matrix products, arithmetic and copies ran while one was open for 3% of the time, Pallas kernels for 16%

profile of v5, /device:TPU:32, one launch (start us, length us, event | category | flops | bytes accessed | tf_op | source)
XLA Modules:
  0.0 174.9 jit_solution(7929125074460389467)
XLA Ops:
  6.5 3.0 %shard_map.128 = (bf16[512,896]{1,0:T(8,128)(2,1)}, bf16[512,256]{1,0:T(8,128)(2,1)}) custom-call(bf16[192,2048]{1,0:T(8,128)(2,1)} %rows_ref.4, f32[1,2048]{1,0:T(1,128)} %bitcast.19, s32[8,192]{1,0:T(8,128)} %bitcast.21), custom_call_target="tpu_custom_call" | custom-call | flops 226492416 | bytes 1980416 | tf_op jit(solution)/shard_map/pallas_call | solution.py:34
  9.6 9.7 %all-to-all-start = ((bf16[32,16,896]{2,1,0:T(8,128)(2,1)}), bf16[32,16,896]{2,1,0:T(8,128)(2,1)S(1)}, u32[]{:S(2)}, u32[]{:S(2)}) async-start(bf16[32,16,896]{2,1,0:T(8,128)(2,1)} %bitcast.26), calls=%async_computation | async-start | bytes 1835008 | tf_op jit(solution)/shard_map/all_to_all | solution.py:320
  19.2 0.0 all-gather.2.cloned.1.call-start
  19.3 0.7 constant_dynamic-slice_fusion.2
  20.0 0.0 copy-done.8
  20.0 0.7 pad_maximum_fusion
  20.7 0.0 all-gather.2.cloned.1.call-update
  20.7 27.2 %all-to-all-done = bf16[32,16,896]{2,1,0:T(8,128)(2,1)S(1)} async-done(((bf16[32,16,896]{2,1,0:T(8,128)(2,1)}), bf16[32,16,896]{2,1,0:T(8,128)(2,1)S(1)}, u32[]{:S(2)}, u32[]{:S(2)}) %all-to-all-start) | async-done | bytes 917536 | tf_op jit(solution)/shard_map/all_to_all | solution.py:320
  48.0 1.6 collective-permute-start
  49.6 3.9 %all-to-all-start.1 = ((bf16[32,16,256]{2,1,0:T(8,128)(2,1)}), bf16[32,16,256]{2,1,0:T(8,128)(2,1)S(1)}, u32[]{:S(2)}, u32[]{:S(2)}) async-start(bf16[32,16,256]{2,1,0:T(8,128)(2,1)} %bitcast.4), calls=%async_computation.1 | async-start | bytes 524288 | tf_op jit(solution)/shard_map/all_to_all | solution.py:320
  53.4 0.0 copy-done.7
  53.4 6.4 %shard_map.129.acc_ref = f32[512,1536]{1,0:T(8,128)} custom-call(bf16[512,896]{1,0:T(8,128)(2,1)} %bitcast.24, bf16[1,2048,1536]{2,1,0:T(8,128)(2,1)} %w_ref.3), custom_call_target="tpu_custom_call" | custom-call | flops 1409286144 | bytes 10354688 | tf_op jit(solution)/shard_map/pallas_call | solution.py:34
  59.9 8.2 %all-gather.2.cloned.1.call-done.near_ref = bf16[512,1280]{1,0:T(8,128)(2,1)} async-done(((bf16[64,1280]{1,0:T(8,128)(2,1)}), bf16[512,1280]{1,0:T(8,128)(2,1)}) %all-gather.2.cloned.1.call-update) | async-done | bytes 1310736 | tf_op jit(solution)/shard_map/all_gather | solution.py:317
  68.1 1.5 collective-permute-start.2
  69.6 0.0 all-to-all-done.1
  69.6 0.0 collective-permute-done.got_ref
  69.6 8.3 %shard_map.130 = (bf16[512,512]{1,0:T(8,128)(2,1)}, bf16[512,768]{1,0:T(8,128)(2,1)S(1)}, bf16[512,768]{1,0:T(8,128)(2,1)}) custom-call(f32[512,1536]{1,0:T(8,128)} %shard_map.129.acc_ref, bf16[512,896]{1,0:T(8,128)(2,1)} %collective-permute-done.got_ref, bf16[512,256]{1,0:T(8,128)(2,1)S(1)} %bitcast.17, bf16[1,2048,1536]{2,1,0:T(8,128)(2,1)} %w_ref.3, ...), custom_call_target="tpu_custom_call" | custom-call | flops 3422552064 | bytes 17170432 | tf_op jit(solution)/shard_map/pallas_call | solution.py:34
  77.8 1.3 collective-permute-start.1
  79.2 5.7 %all-to-all-start.3 = ((bf16[32,16,512]{2,1,0:T(8,128)(2,1)}), bf16[32,16,512]{2,1,0:T(8,128)(2,1)S(1)}, u32[]{:S(2)}, u32[]{:S(2)}) async-start(bf16[32,16,512]{2,1,0:T(8,128)(2,1)} %bitcast.8), calls=%async_computation.3 | async-start | bytes 1048576 | tf_op jit(solution)/shard_map/all_to_all | solution.py:320
  84.8 0.2 collective-permute-start.3
  85.1 4.1 %shard_map.131 = bf16[512,768]{1,0:T(8,128)(2,1)} custom-call(bf16[512,768]{1,0:T(8,128)(2,1)} %get-tuple-element.17.hidden_ref, bf16[1,768,2048]{2,1,0:T(8,128)(2,1)} %down_ref.3), custom_call_target="tpu_custom_call" | custom-call | tf_op jit(solution)/shard_map/pallas_call | solution.py:34
  89.2 6.7 %collective-permute-done.1 = bf16[512,768]{1,0:T(8,128)(2,1)S(1)} collective-permute-done((bf16[512,768]{1,0:T(8,128)(2,1)S(1)}, bf16[512,768]{1,0:T(8,128)(2,1)S(1)}, u32[]{:S(2)}, u32[]{:S(2)}) %collective-permute-start.1) | collective-permute-done | bytes 786464 | tf_op jit(solution)/shard_map/ppermute | solution.py:323
  95.9 2.2 %add_convert_fusion.after_ref = bf16[512,768]{1,0:T(8,128)(2,1)} fusion(bf16[512,768]{1,0:T(8,128)(2,1)S(1)} %collective-permute-done.1, bf16[512,768]{1,0:T(8,128)(2,1)} %shard_map.131), kind=kLoop, calls=%fused_computation | loop fusion | flops 1572864 | bytes 2359296 | tf_op jit(solution)/shard_map/convert_element_type | solution.py:391
  98.1 2.4 %collective-permute-done.2.value_ref = bf16[512,1280]{1,0:T(8,128)(2,1)S(1)} collective-permute-done((bf16[512,1280]{1,0:T(8,128)(2,1)}, bf16[512,1280]{1,0:T(8,128)(2,1)S(1)}, u32[]{:S(2)}, u32[]{:S(2)}) %collective-permute-start.2) | collective-permute-done | bytes 1310752 | tf_op jit(solution)/shard_map/ppermute | solution.py:386
  100.5 0.0 collective-permute-start.4
  100.5 2.1 %all-to-all-done.3 = bf16[32,16,512]{2,1,0:T(8,128)(2,1)S(1)} async-done(((bf16[32,16,512]{2,1,0:T(8,128)(2,1)}), bf16[32,16,512]{2,1,0:T(8,128)(2,1)S(1)}, u32[]{:S(2)}, u32[]{:S(2)}) %all-to-all-start.3) | async-done | bytes 524320 | tf_op jit(solution)/shard_map/all_to_all | solution.py:320
  102.6 6.6 %all-to-all-start.2 = ((bf16[32,16,768]{2,1,0:T(8,128)(2,1)}), bf16[32,16,768]{2,1,0:T(8,128)(2,1)S(1)}, u32[]{:S(2)}, u32[]{:S(2)}) async-start(bf16[32,16,768]{2,1,0:T(8,128)(2,1)} %bitcast.6), calls=%async_computation.2 | async-start | bytes 1572864 | tf_op jit(solution)/shard_map/all_to_all | solution.py:320
  109.2 0.4 fusion.3
  109.6 0.8 pad_maximum_fusion.1
  110.4 0.0 collective-permute-done.3.other_near_ref
  110.4 0.0 collective-permute-done.4.other_across_ref
  110.4 0.0 copy-done
  110.4 0.0 copy-start.1
  110.4 0.0 copy-start.5
  110.4 0.0 copy-start.6
  110.4 7.4 %shard_map.133 = (bf16[192,768]{1,0:T(8,128)(2,1)}, f32[192,768]{1,0:T(8,128)}, f32[192,512]{1,0:T(8,128)}) custom-call(bf16[192,2048]{1,0:T(8,128)(2,1)} %rows_ref.5, f32[1,2048]{1,0:T(1,128)} %bitcast.27, bf16[512,1280]{1,0:T(8,128)(2,1)} %all-gather.2.cloned.1.call-done.near_ref, bf16[512,1280]{1,0:T(8,128)(2,1)} %copy-done, ...), custom_call_target="tpu_custom_call" | custom-call | tf_op jit(solution)/shard_map/pallas_call | solution.py:34
  117.9 0.8 collective-permute-start.5
  118.7 1.0 copy-done.3
  119.7 1.1 shard_map.127.map_ref
  120.9 0.9 constant_dynamic-slice_fusion.own_ref
  121.8 10.8 %all-to-all-done.2 = bf16[32,16,768]{2,1,0:T(8,128)(2,1)S(1)} async-done(((bf16[32,16,768]{2,1,0:T(8,128)(2,1)}), bf16[32,16,768]{2,1,0:T(8,128)(2,1)S(1)}, u32[]{:S(2)}, u32[]{:S(2)}) %all-to-all-start.2) | async-done | bytes 786464 | tf_op jit(solution)/shard_map/all_to_all | solution.py:320
  132.5 0.0 collective-permute-done.5.got_ref
  132.6 1.4 shard_map.134
  134.0 17.3 %all_to_all.54 = bf16[8,24,1280]{2,1,0:T(8,128)(2,1)S(1)} all-to-all(bf16[8,24,1280]{2,1,0:T(8,128)(2,1)S(1)} %bitcast.18), channel_id=1, replica_groups=mesh['ep'=32,'tp'=8] {'tp'}, dimensions={0} | all-to-all | bytes 983040 | tf_op jit(solution)/shard_map/all_to_all | solution.py:451
  151.3 0.1 convert_element_type.22
  151.5 0.1 broadcast_in_dim.24
  151.5 15.7 %all_to_all.55 = bf16[8,24,2048]{2,1,0:T(8,128)(2,1)S(1)} all-to-all(bf16[8,24,2048]{2,1,0:T(8,128)(2,1)S(1)} %broadcast_in_dim.24), channel_id=1, replica_groups=mesh['ep'=32,'tp'=8] {'tp'}, dimensions={0} | all-to-all | bytes 1572864 | tf_op jit(solution)/shard_map/all_to_all | solution.py:462
  167.2 0.9 copy.19
  (18 shorter events, 0.1 us)
Async XLA Ops:
  6.5 13.5 %copy-start.9 = (bf16[64,512]{1,0:T(8,128)(2,1)S(1)}, bf16[64,512]{1,0:T(8,128)(2,1)}, u32[]{:S(2)}) copy-start(bf16[64,512]{1,0:T(8,128)(2,1)} %param.17) | copy-start | bytes 196612
  6.5 13.5 %copy-start.8 = (bf16[64,512]{1,0:T(8,128)(2,1)S(1)}, bf16[64,512]{1,0:T(8,128)(2,1)}, u32[]{:S(2)}) copy-start(bf16[64,512]{1,0:T(8,128)(2,1)} %param.19) | copy-start | bytes 196612
  9.6 38.4 %all-to-all-start = ((bf16[32,16,896]{2,1,0:T(8,128)(2,1)}), bf16[32,16,896]{2,1,0:T(8,128)(2,1)S(1)}, u32[]{:S(2)}, u32[]{:S(2)}) async-start(bf16[32,16,896]{2,1,0:T(8,128)(2,1)} %bitcast.26), calls=%async_computation | async-start | bytes 1835008 | tf_op jit(solution)/shard_map/all_to_all | solution.py:320
  19.2 48.9 %all-gather.2.cloned.1.call-start = ((), (), s32[]{:S(2)}) async-start(), calls=%async_computation.6 | async-start | bytes 1474560 | tf_op jit(solution)/shard_map/all_gather | solution.py:317
  48.0 5.4 %copy-start.7 = (bf16[32,16,896]{2,1,0:T(8,128)(2,1)}, bf16[32,16,896]{2,1,0:T(8,128)(2,1)S(1)}, u32[]{:S(2)}) copy-start(bf16[32,16,896]{2,1,0:T(8,128)(2,1)S(1)} %all-to-all-done) | copy-start | bytes 2752516
  48.0 21.6 %collective-permute-start = (bf16[512,896]{1,0:T(8,128)(2,1)S(1)}, bf16[512,896]{1,0:T(8,128)(2,1)}, u32[]{:S(2)}, u32[]{:S(2)}) collective-permute-start(bf16[512,896]{1,0:T(8,128)(2,1)S(1)} %bitcast.23), channel_id=1, source_target_pairs={{0,1},{1,0},{2,3},{3,2},{4,5},{5,4},{6,7},{7,6},{8,9},{9,8},{10,11... | collective-permute-start | bytes 2752520 | tf_op jit(solution)/shard_map/ppermute | solution.py:323
  49.6 20.0 %all-to-all-start.1 = ((bf16[32,16,256]{2,1,0:T(8,128)(2,1)}), bf16[32,16,256]{2,1,0:T(8,128)(2,1)S(1)}, u32[]{:S(2)}, u32[]{:S(2)}) async-start(bf16[32,16,256]{2,1,0:T(8,128)(2,1)} %bitcast.4), calls=%async_computation.1 | async-start | bytes 524288 | tf_op jit(solution)/shard_map/all_to_all | solution.py:320
  68.1 32.4 %collective-permute-start.2 = (bf16[512,1280]{1,0:T(8,128)(2,1)}, bf16[512,1280]{1,0:T(8,128)(2,1)S(1)}, u32[]{:S(2)}, u32[]{:S(2)}) collective-permute-start(bf16[512,1280]{1,0:T(8,128)(2,1)} %all-gather.2.cloned.1.call-done.near_ref), channel_id=1, source_target_pairs={{0,128},{8,136},{16,144},{24,152},{32,160},{40,168},{48,176},{56,1... | collective-permute-start | bytes 3932168 | tf_op jit(solution)/shard_map/ppermute | solution.py:386
  77.8 18.0 %collective-permute-start.1 = (bf16[512,768]{1,0:T(8,128)(2,1)S(1)}, bf16[512,768]{1,0:T(8,128)(2,1)S(1)}, u32[]{:S(2)}, u32[]{:S(2)}) collective-permute-start(bf16[512,768]{1,0:T(8,128)(2,1)S(1)} %get-tuple-element.18), channel_id=1, source_target_pairs={{0,1},{1,0},{2,3},{3,2},{4,5},{5,4},{6,7},{7,6},{8,9},{9,8},{10,11... | collective-permute-start | bytes 2359304 | tf_op jit(solution)/shard_map/ppermute | solution.py:323
  79.2 23.4 %all-to-all-start.3 = ((bf16[32,16,512]{2,1,0:T(8,128)(2,1)}), bf16[32,16,512]{2,1,0:T(8,128)(2,1)S(1)}, u32[]{:S(2)}, u32[]{:S(2)}) async-start(bf16[32,16,512]{2,1,0:T(8,128)(2,1)} %bitcast.8), calls=%async_computation.3 | async-start | bytes 1048576 | tf_op jit(solution)/shard_map/all_to_all | solution.py:320
  84.8 25.6 %collective-permute-start.3 = (bf16[512,1280]{1,0:T(8,128)(2,1)}, bf16[512,1280]{1,0:T(8,128)(2,1)}, u32[]{:S(2)}, u32[]{:S(2)}) collective-permute-start(bf16[512,1280]{1,0:T(8,128)(2,1)} %all-gather.2.cloned.1.call-done.near_ref), channel_id=1, source_target_pairs={{0,8},{8,0},{16,24},{24,16},{32,40},{40,32},{48,56},{56,48},{64,72... | collective-permute-start | bytes 3932168 | tf_op jit(solution)/shard_map/ppermute | solution.py:388
  100.5 9.9 %copy-start = (bf16[512,1280]{1,0:T(8,128)(2,1)}, bf16[512,1280]{1,0:T(8,128)(2,1)S(1)}, u32[]{:S(2)}) copy-start(bf16[512,1280]{1,0:T(8,128)(2,1)S(1)} %shard_map.132.across_ref) | copy-start | bytes 3932164
  100.5 9.9 %collective-permute-start.4 = (bf16[512,1280]{1,0:T(8,128)(2,1)S(1)}, bf16[512,1280]{1,0:T(8,128)(2,1)}, u32[]{:S(2)}, u32[]{:S(2)}) collective-permute-start(bf16[512,1280]{1,0:T(8,128)(2,1)S(1)} %shard_map.132.across_ref), channel_id=1, source_target_pairs={{0,8},{8,0},{16,24},{24,16},{32,40},{40,32},{48,56},{56,48},{64,72... | collective-permute-start | bytes 3932168 | tf_op jit(solution)/shard_map/ppermute | solution.py:404
  102.6 30.0 %all-to-all-start.2 = ((bf16[32,16,768]{2,1,0:T(8,128)(2,1)}), bf16[32,16,768]{2,1,0:T(8,128)(2,1)S(1)}, u32[]{:S(2)}, u32[]{:S(2)}) async-start(bf16[32,16,768]{2,1,0:T(8,128)(2,1)} %bitcast.6), calls=%async_computation.2 | async-start | bytes 1572864 | tf_op jit(solution)/shard_map/all_to_all | solution.py:320
  110.4 8.3 %copy-start.1 = (bf16[192,2048]{1,0:T(8,128)(2,1)S(1)}, bf16[192,2048]{1,0:T(8,128)(2,1)}, u32[]{:S(2)}) copy-start(bf16[192,2048]{1,0:T(8,128)(2,1)} %rows_ref.4) | copy-start | bytes 2359300
  110.4 8.3 %copy-start.5 = (f32[2048]{0:T(1024)S(1)}, f32[2048]{0:T(1024)}, u32[]{:S(2)}) copy-start(f32[2048]{0:T(1024)} %param.16) | copy-start | bytes 24580
  110.4 8.3 %copy-start.6 = (s32[192,8]{0,1:T(8,128)S(1)}, s32[192,8]{0,1:T(8,128)}, u32[]{:S(2)}) copy-start(s32[192,8]{0,1:T(8,128)} %param.23) | copy-start | bytes 18436
  117.9 14.7 %copy-start.2 = (f32[192,768]{1,0:T(8,128)S(1)}, f32[192,768]{1,0:T(8,128)}, u32[]{:S(2)}) copy-start(f32[192,768]{1,0:T(8,128)} %get-tuple-element.20.kept_ref) | copy-start | bytes 1769476
  117.9 14.7 %collective-permute-start.5 = (bf16[192,768]{1,0:T(8,128)(2,1)}, bf16[192,768]{1,0:T(8,128)(2,1)}, u32[]{:S(2)}, u32[]{:S(2)}) collective-permute-start(bf16[192,768]{1,0:T(8,128)(2,1)} %get-tuple-element.21), channel_id=1, source_target_pairs={{0,1},{1,0},{2,3},{3,2},{4,5},{5,4},{6,7},{7,6},{8,9},{9,8},{10,11... | collective-permute-start | bytes 884744 | tf_op jit(solution)/shard_map/ppermute | solution.py:323
  118.7 1.0 copy-start.3
  119.7 12.8 %copy-start.4 = (f32[192,512]{1,0:T(8,128)S(1)}, f32[192,512]{1,0:T(8,128)}, u32[]{:S(2)}) copy-start(f32[192,512]{1,0:T(8,128)} %get-tuple-element.22.direct_ref) | copy-start | bytes 1179652
Sparse Core Ops, SparseCore 0:
  21.8 46.2 all-gather.1

commit v6 on v4

--- a/solution.py
+++ b/solution.py
@@ -109,7 +109,9 @@
     copy = pltpu.make_async_copy(w_ref.at[0, pl.ds(mine, width)], w_buf, sem)
     copy.start()
     copy.wait()
-    out_ref[...] = jnp.dot(own_ref[...], w_buf[...], preferred_element_type=F32)
+    out_ref[...] = jnp.dot(
+        own_ref[...], w_buf[...], preferred_element_type=F32
+    ).astype(BF16)
 
 
 def expert_body(
@@ -164,7 +166,7 @@
     def product(columns):
         got = jnp.dot(got_ref[...], w_buf[:split, columns], preferred_element_type=F32)
         both = jnp.dot(both_ref[...], w_buf[split:, columns], preferred_element_type=F32)
-        return acc[:, columns] + got + both
+        return acc[:, columns].astype(F32) + got + both
 
     for step, strip in enumerate(strips):
         for copy in strip:
@@ -345,7 +347,7 @@
     )
     (acc,) = call(
         first_part_body,
-        [jax.ShapeDtypeStruct((places, ff2), F32)],
+        [jax.ShapeDtypeStruct((places, ff2), BF16)],
         (arrived, gate_up_weight),
         2 * places * shared_in * ff2,
         specs=[vmem(), anywhere()],
@@ -364,7 +366,7 @@
         specs=[anywhere(), vmem(), vmem()] + [anywhere()] * 3,
         out_specs=[anywhere()] * 3,
         scratch=[
-            pltpu.VMEM((places, ff2), F32),
+            pltpu.VMEM((places, ff2), BF16),
             pltpu.VMEM((shared_in + direct_in, ff2), BF16),
             pltpu.VMEM((ff, shared + direct), BF16),
             pltpu.VMEM((places, ff), BF16),

time: 176 us -> 176 us (level)
  transfers between devices with their start and end apart: 11 -> 11, of which waited for: 6 -> 6; matrix products, arithmetic and copies ran while one was open for 3% -> 3% of each run, Pallas kernels for 17% -> 16%
where the time goes in v6:
time: 176 us; the launch traced here: 175 us
  waiting for transfers between devices  56.9 us (32%)
  blocking collectives  33 us (19%)
  Pallas kernels  32 us (18%)
  starting transfers between devices  31.5 us (18%)
  between operations  13.6 us (8%)
  other arithmetic  4.49 us (3%)
  local copies, waits for them, and re-layouts  3.54 us (2%)
    all_to_all x4, waiting for transfers between devices, to_owners(): return lax.all_to_all(value, 'ep', split_axis=0, concat_axis=0, tiled=True)  39 us
    pallas_call x8, Pallas kernels, call(): pl.pallas_call(body, out_shape=out_shape, in_specs=specs or [vmem()] * le...  32 us
    all_to_all x4, starting transfers between devices, to_owners(): return lax.all_to_all(value, 'ep', split_axis=0, concat_axis=0, tiled=True)  25.9 us
    all_to_all x1, blocking collectives, local(): lax.all_to_all(total.reshape(n_tp, share, shared + direct), 'tp', split_a...  17.3 us
    all_to_all x1, blocking collectives, local(): lax.all_to_all(jnp.broadcast_to(mine[None], (n_tp, share, d_model)), 'tp'...  15.7 us
    all_gather x1, waiting for transfers between devices, local(): lax.all_gather(packed, 'ep', axis=0, tiled=True, axis_index_groups=along_z)  8.73 us
    ppermute x3, waiting for transfers between devices, swapped(): return lax.ppermute(value, 'tp', partner)  6.83 us
    ppermute x3, starting transfers between devices, swapped(): return lax.ppermute(value, 'tp', partner)  3.8 us
  transfers between devices with their start and end apart: 11, of which 6 were waited for; matrix products, arithmetic and copies ran while one was open for 3% of the time, Pallas kernels for 16%

profile of v6, /device:TPU:32, one launch (start us, length us, event | category | flops | bytes accessed | tf_op | source)
XLA Modules:
  0.0 174.9 jit_solution(14458235010903100966)
XLA Ops:
  6.5 3.0 %shard_map.128 = (bf16[512,896]{1,0:T(8,128)(2,1)}, bf16[512,256]{1,0:T(8,128)(2,1)}) custom-call(bf16[192,2048]{1,0:T(8,128)(2,1)} %rows_ref.4, f32[1,2048]{1,0:T(1,128)} %bitcast.24, s32[8,192]{1,0:T(8,128)} %bitcast.26), custom_call_target="tpu_custom_call" | custom-call | flops 226492416 | bytes 1980416 | tf_op jit(solution)/shard_map/pallas_call | solution.py:34
  9.6 9.7 %all-to-all-start = ((bf16[32,16,896]{2,1,0:T(8,128)(2,1)}), bf16[32,16,896]{2,1,0:T(8,128)(2,1)S(1)}, u32[]{:S(2)}, u32[]{:S(2)}) async-start(bf16[32,16,896]{2,1,0:T(8,128)(2,1)} %bitcast.22), calls=%async_computation | async-start | bytes 1835008 | tf_op jit(solution)/shard_map/all_to_all | solution.py:322
  19.2 0.0 all-gather.2.cloned.1.call-start
  19.3 0.7 constant_dynamic-slice_fusion.2
  20.0 0.0 copy-done.6
  20.0 0.0 copy-done.5
  20.0 0.7 pad_maximum_fusion
  20.7 0.0 all-gather.2.cloned.1.call-update
  20.8 27.2 %all-to-all-done = bf16[32,16,896]{2,1,0:T(8,128)(2,1)S(1)} async-done(((bf16[32,16,896]{2,1,0:T(8,128)(2,1)}), bf16[32,16,896]{2,1,0:T(8,128)(2,1)S(1)}, u32[]{:S(2)}, u32[]{:S(2)}) %all-to-all-start) | async-done | bytes 917536 | tf_op jit(solution)/shard_map/all_to_all | solution.py:322
  48.0 1.6 collective-permute-start
  49.6 3.9 %all-to-all-start.1 = ((bf16[32,16,256]{2,1,0:T(8,128)(2,1)}), bf16[32,16,256]{2,1,0:T(8,128)(2,1)S(1)}, u32[]{:S(2)}, u32[]{:S(2)}) async-start(bf16[32,16,256]{2,1,0:T(8,128)(2,1)} %bitcast.4), calls=%async_computation.1 | async-start | bytes 524288 | tf_op jit(solution)/shard_map/all_to_all | solution.py:322
  53.4 0.0 copy-done.4
  53.4 5.9 %shard_map.129.acc_ref = bf16[512,1536]{1,0:T(8,128)(2,1)} custom-call(bf16[512,896]{1,0:T(8,128)(2,1)} %bitcast.20, bf16[1,2048,1536]{2,1,0:T(8,128)(2,1)} %w_ref.3), custom_call_target="tpu_custom_call" | custom-call | flops 1409286144 | bytes 8781824 | tf_op jit(solution)/shard_map/pallas_call | solution.py:34
  59.4 8.7 %all-gather.2.cloned.1.call-done.near_ref = bf16[512,1280]{1,0:T(8,128)(2,1)} async-done(((bf16[64,1280]{1,0:T(8,128)(2,1)}), bf16[512,1280]{1,0:T(8,128)(2,1)}) %all-gather.2.cloned.1.call-update) | async-done | bytes 1310736 | tf_op jit(solution)/shard_map/all_gather | solution.py:319
  68.1 1.5 collective-permute-start.2
  69.6 0.0 all-to-all-done.1
  69.6 0.0 collective-permute-done.got_ref
  69.6 8.1 %shard_map.130 = (bf16[512,512]{1,0:T(8,128)(2,1)}, bf16[512,768]{1,0:T(8,128)(2,1)S(1)}, bf16[512,768]{1,0:T(8,128)(2,1)}) custom-call(bf16[512,1536]{1,0:T(8,128)(2,1)} %shard_map.129.acc_ref, bf16[512,896]{1,0:T(8,128)(2,1)} %collective-permute-done.got_ref, bf16[512,256]{1,0:T(8,128)(2,1)S(1)} %bitcast.17, bf16[1,2048,1536]{2,1,0:T(8,128)(2,1)} %w_ref.3, ...), custom_call_target="tpu_custom_call" | custom-call | flops 3422552064 | bytes 15597568 | tf_op jit(solution)/shard_map/pallas_call | solution.py:34
  77.7 1.3 collective-permute-start.1
  79.0 5.7 %all-to-all-start.3 = ((bf16[32,16,512]{2,1,0:T(8,128)(2,1)}), bf16[32,16,512]{2,1,0:T(8,128)(2,1)S(1)}, u32[]{:S(2)}, u32[]{:S(2)}) async-start(bf16[32,16,512]{2,1,0:T(8,128)(2,1)} %bitcast.8), calls=%async_computation.3 | async-start | bytes 1048576 | tf_op jit(solution)/shard_map/all_to_all | solution.py:322
  84.6 0.2 collective-permute-start.3
  84.9 4.1 %shard_map.131 = bf16[512,768]{1,0:T(8,128)(2,1)} custom-call(bf16[512,768]{1,0:T(8,128)(2,1)} %get-tuple-element.17.hidden_ref, bf16[1,768,2048]{2,1,0:T(8,128)(2,1)} %down_ref.3), custom_call_target="tpu_custom_call" | custom-call | tf_op jit(solution)/shard_map/pallas_call | solution.py:34
  89.0 6.8 %collective-permute-done.1 = bf16[512,768]{1,0:T(8,128)(2,1)} collective-permute-done((bf16[512,768]{1,0:T(8,128)(2,1)S(1)}, bf16[512,768]{1,0:T(8,128)(2,1)}, u32[]{:S(2)}, u32[]{:S(2)}) %collective-permute-start.1) | collective-permute-done | bytes 786464 | tf_op jit(solution)/shard_map/ppermute | solution.py:325
  95.8 2.4 %add_convert_fusion.after_ref = bf16[512,768]{1,0:T(8,128)(2,1)} fusion(bf16[512,768]{1,0:T(8,128)(2,1)} %collective-permute-done.1, bf16[512,768]{1,0:T(8,128)(2,1)} %shard_map.131), kind=kLoop, calls=%fused_computation | loop fusion | flops 1572864 | bytes 2359296 | tf_op jit(solution)/shard_map/convert_element_type | solution.py:392
  98.2 2.2 %collective-permute-done.2.value_ref = bf16[512,1280]{1,0:T(8,128)(2,1)S(1)} collective-permute-done((bf16[512,1280]{1,0:T(8,128)(2,1)}, bf16[512,1280]{1,0:T(8,128)(2,1)S(1)}, u32[]{:S(2)}, u32[]{:S(2)}) %collective-permute-start.2) | collective-permute-done | bytes 1310752 | tf_op jit(solution)/shard_map/ppermute | solution.py:387
  100.5 0.0 collective-permute-start.4
  100.5 1.9 %all-to-all-done.3 = bf16[32,16,512]{2,1,0:T(8,128)(2,1)S(1)} async-done(((bf16[32,16,512]{2,1,0:T(8,128)(2,1)}), bf16[32,16,512]{2,1,0:T(8,128)(2,1)S(1)}, u32[]{:S(2)}, u32[]{:S(2)}) %all-to-all-start.3) | async-done | bytes 524320 | tf_op jit(solution)/shard_map/all_to_all | solution.py:322
  102.4 6.8 %all-to-all-start.2 = ((bf16[32,16,768]{2,1,0:T(8,128)(2,1)}), bf16[32,16,768]{2,1,0:T(8,128)(2,1)S(1)}, u32[]{:S(2)}, u32[]{:S(2)}) async-start(bf16[32,16,768]{2,1,0:T(8,128)(2,1)} %bitcast.6), calls=%async_computation.2 | async-start | bytes 1572864 | tf_op jit(solution)/shard_map/all_to_all | solution.py:322
  109.2 0.4 fusion.3
  109.6 0.8 pad_maximum_fusion.1
  110.4 0.0 collective-permute-done.3.other_near_ref
  110.4 0.0 collective-permute-done.4.other_across_ref
  110.4 0.0 copy-done
  110.4 7.4 %shard_map.133 = (bf16[192,768]{1,0:T(8,128)(2,1)}, f32[192,768]{1,0:T(8,128)}, f32[192,512]{1,0:T(8,128)}) custom-call(bf16[192,2048]{1,0:T(8,128)(2,1)} %rows_ref.5, f32[1,2048]{1,0:T(1,128)} %bitcast.23, bf16[512,1280]{1,0:T(8,128)(2,1)} %all-gather.2.cloned.1.call-done.near_ref, bf16[512,1280]{1,0:T(8,128)(2,1)} %copy-done, ...), custom_call_target="tpu_custom_call" | custom-call | tf_op jit(solution)/shard_map/pallas_call | solution.py:34
  117.8 0.9 collective-permute-start.5
  118.7 3.1 %shard_map.127.map_ref = bf16[192,512]{1,0:T(8,128)(2,1)} custom-call(bf16[192,2048]{1,0:T(8,128)(2,1)} %rows_ref.4, f32[1,2048]{1,0:T(1,128)} %bitcast.25, bf16[128,2048]{1,0:T(8,128)(2,1)} %router_ref.1, s32[8,192]{1,0:T(8,128)} %bitcast.27), custom_call_target="tpu_custom_call" | custom-call | tf_op jit(solution)/shard_map/pallas_call | solution.py:34
  121.8 0.9 constant_dynamic-slice_fusion.own_ref
  122.7 9.9 %all-to-all-done.2 = bf16[32,16,768]{2,1,0:T(8,128)(2,1)S(1)} async-done(((bf16[32,16,768]{2,1,0:T(8,128)(2,1)}), bf16[32,16,768]{2,1,0:T(8,128)(2,1)S(1)}, u32[]{:S(2)}, u32[]{:S(2)}) %all-to-all-start.2) | async-done | bytes 786464 | tf_op jit(solution)/shard_map/all_to_all | solution.py:322
  132.5 0.0 collective-permute-done.5.got_ref
  132.6 0.0 copy-done.2
  132.6 0.0 copy-done.3
  132.6 0.9 copy-done.1
  133.5 0.4 shard_map.134
  133.9 17.3 %all_to_all.54 = bf16[8,24,1280]{2,1,0:T(8,128)(2,1)S(1)} all-to-all(bf16[8,24,1280]{2,1,0:T(8,128)(2,1)S(1)} %bitcast.18), channel_id=1, replica_groups=mesh['ep'=32,'tp'=8] {'tp'}, dimensions={0} | all-to-all | bytes 983040 | tf_op jit(solution)/shard_map/all_to_all | solution.py:452
  151.3 0.1 convert_element_type.22
  151.4 0.1 broadcast_in_dim.24
  151.5 15.7 %all_to_all.55 = bf16[8,24,2048]{2,1,0:T(8,128)(2,1)S(1)} all-to-all(bf16[8,24,2048]{2,1,0:T(8,128)(2,1)S(1)} %broadcast_in_dim.24), channel_id=1, replica_groups=mesh['ep'=32,'tp'=8] {'tp'}, dimensions={0} | all-to-all | bytes 1572864 | tf_op jit(solution)/shard_map/all_to_all | solution.py:463
  167.2 0.9 copy.19
  (12 shorter events, 0.1 us)
Async XLA Ops:
  6.5 13.5 %copy-start.6 = (bf16[64,512]{1,0:T(8,128)(2,1)S(1)}, bf16[64,512]{1,0:T(8,128)(2,1)}, u32[]{:S(2)}) copy-start(bf16[64,512]{1,0:T(8,128)(2,1)} %param.17) | copy-start | bytes 196612
  6.5 13.5 %copy-start.5 = (bf16[64,512]{1,0:T(8,128)(2,1)S(1)}, bf16[64,512]{1,0:T(8,128)(2,1)}, u32[]{:S(2)}) copy-start(bf16[64,512]{1,0:T(8,128)(2,1)} %param.19) | copy-start | bytes 196612
  9.6 38.4 %all-to-all-start = ((bf16[32,16,896]{2,1,0:T(8,128)(2,1)}), bf16[32,16,896]{2,1,0:T(8,128)(2,1)S(1)}, u32[]{:S(2)}, u32[]{:S(2)}) async-start(bf16[32,16,896]{2,1,0:T(8,128)(2,1)} %bitcast.22), calls=%async_computation | async-start | bytes 1835008 | tf_op jit(solution)/shard_map/all_to_all | solution.py:322
  19.2 48.9 %all-gather.2.cloned.1.call-start = ((), (), s32[]{:S(2)}) async-start(), calls=%async_computation.6 | async-start | bytes 1474560 | tf_op jit(solution)/shard_map/all_gather | solution.py:319
  48.0 5.4 %copy-start.4 = (bf16[32,16,896]{2,1,0:T(8,128)(2,1)}, bf16[32,16,896]{2,1,0:T(8,128)(2,1)S(1)}, u32[]{:S(2)}) copy-start(bf16[32,16,896]{2,1,0:T(8,128)(2,1)S(1)} %all-to-all-done) | copy-start | bytes 2752516
  48.0 21.6 %collective-permute-start = (bf16[512,896]{1,0:T(8,128)(2,1)S(1)}, bf16[512,896]{1,0:T(8,128)(2,1)}, u32[]{:S(2)}, u32[]{:S(2)}) collective-permute-start(bf16[512,896]{1,0:T(8,128)(2,1)S(1)} %bitcast.19), channel_id=1, source_target_pairs={{0,1},{1,0},{2,3},{3,2},{4,5},{5,4},{6,7},{7,6},{8,9},{9,8},{10,11... | collective-permute-start | bytes 2752520 | tf_op jit(solution)/shard_map/ppermute | solution.py:325
  49.6 20.0 %all-to-all-start.1 = ((bf16[32,16,256]{2,1,0:T(8,128)(2,1)}), bf16[32,16,256]{2,1,0:T(8,128)(2,1)S(1)}, u32[]{:S(2)}, u32[]{:S(2)}) async-start(bf16[32,16,256]{2,1,0:T(8,128)(2,1)} %bitcast.4), calls=%async_computation.1 | async-start | bytes 524288 | tf_op jit(solution)/shard_map/all_to_all | solution.py:322
  68.1 32.4 %collective-permute-start.2 = (bf16[512,1280]{1,0:T(8,128)(2,1)}, bf16[512,1280]{1,0:T(8,128)(2,1)S(1)}, u32[]{:S(2)}, u32[]{:S(2)}) collective-permute-start(bf16[512,1280]{1,0:T(8,128)(2,1)} %all-gather.2.cloned.1.call-done.near_ref), channel_id=1, source_target_pairs={{0,128},{8,136},{16,144},{24,152},{32,160},{40,168},{48,176},{56,1... | collective-permute-start | bytes 3932168 | tf_op jit(solution)/shard_map/ppermute | solution.py:387
  77.7 18.1 %collective-permute-start.1 = (bf16[512,768]{1,0:T(8,128)(2,1)S(1)}, bf16[512,768]{1,0:T(8,128)(2,1)}, u32[]{:S(2)}, u32[]{:S(2)}) collective-permute-start(bf16[512,768]{1,0:T(8,128)(2,1)S(1)} %get-tuple-element.18), channel_id=1, source_target_pairs={{0,1},{1,0},{2,3},{3,2},{4,5},{5,4},{6,7},{7,6},{8,9},{9,8},{10,11... | collective-permute-start | bytes 2359304 | tf_op jit(solution)/shard_map/ppermute | solution.py:325
  79.0 23.4 %all-to-all-start.3 = ((bf16[32,16,512]{2,1,0:T(8,128)(2,1)}), bf16[32,16,512]{2,1,0:T(8,128)(2,1)S(1)}, u32[]{:S(2)}, u32[]{:S(2)}) async-start(bf16[32,16,512]{2,1,0:T(8,128)(2,1)} %bitcast.8), calls=%async_computation.3 | async-start | bytes 1048576 | tf_op jit(solution)/shard_map/all_to_all | solution.py:322
  84.6 25.8 %collective-permute-start.3 = (bf16[512,1280]{1,0:T(8,128)(2,1)}, bf16[512,1280]{1,0:T(8,128)(2,1)}, u32[]{:S(2)}, u32[]{:S(2)}) collective-permute-start(bf16[512,1280]{1,0:T(8,128)(2,1)} %all-gather.2.cloned.1.call-done.near_ref), channel_id=1, source_target_pairs={{0,8},{8,0},{16,24},{24,16},{32,40},{40,32},{48,56},{56,48},{64,72... | collective-permute-start | bytes 3932168 | tf_op jit(solution)/shard_map/ppermute | solution.py:389
  100.5 10.0 %copy-start = (bf16[512,1280]{1,0:T(8,128)(2,1)}, bf16[512,1280]{1,0:T(8,128)(2,1)S(1)}, u32[]{:S(2)}) copy-start(bf16[512,1280]{1,0:T(8,128)(2,1)S(1)} %shard_map.132.across_ref) | copy-start | bytes 3932164
  100.5 10.0 %collective-permute-start.4 = (bf16[512,1280]{1,0:T(8,128)(2,1)S(1)}, bf16[512,1280]{1,0:T(8,128)(2,1)}, u32[]{:S(2)}, u32[]{:S(2)}) collective-permute-start(bf16[512,1280]{1,0:T(8,128)(2,1)S(1)} %shard_map.132.across_ref), channel_id=1, source_target_pairs={{0,8},{8,0},{16,24},{24,16},{32,40},{40,32},{48,56},{56,48},{64,72... | collective-permute-start | bytes 3932168 | tf_op jit(solution)/shard_map/ppermute | solution.py:405
  102.4 30.1 %all-to-all-start.2 = ((bf16[32,16,768]{2,1,0:T(8,128)(2,1)}), bf16[32,16,768]{2,1,0:T(8,128)(2,1)S(1)}, u32[]{:S(2)}, u32[]{:S(2)}) async-start(bf16[32,16,768]{2,1,0:T(8,128)(2,1)} %bitcast.6), calls=%async_computation.2 | async-start | bytes 1572864 | tf_op jit(solution)/shard_map/all_to_all | solution.py:322
  117.8 14.7 %copy-start.2 = (f32[192,768]{1,0:T(8,128)S(1)}, f32[192,768]{1,0:T(8,128)}, u32[]{:S(2)}) copy-start(f32[192,768]{1,0:T(8,128)} %get-tuple-element.20.kept_ref) | copy-start | bytes 1769476
  117.8 14.7 %copy-start.3 = (f32[192,512]{1,0:T(8,128)S(1)}, f32[192,512]{1,0:T(8,128)}, u32[]{:S(2)}) copy-start(f32[192,512]{1,0:T(8,128)} %get-tuple-element.22.direct_ref) | copy-start | bytes 1179652
  117.8 14.7 %collective-permute-start.5 = (bf16[192,768]{1,0:T(8,128)(2,1)}, bf16[192,768]{1,0:T(8,128)(2,1)S(1)}, u32[]{:S(2)}, u32[]{:S(2)}) collective-permute-start(bf16[192,768]{1,0:T(8,128)(2,1)} %get-tuple-element.21), channel_id=1, source_target_pairs={{0,1},{1,0},{2,3},{3,2},{4,5},{5,4},{6,7},{7,6},{8,9},{9,8},{10,11... | collective-permute-start | bytes 884744 | tf_op jit(solution)/shard_map/ppermute | solution.py:325
  132.6 0.9 copy-start.1
Sparse Core Ops, SparseCore 0:
  21.8 46.2 all-gather.1
